TPU v7x, 128 devices: a whole 4x4x4 slice. The times are simulated.
128 devices in a mesh: pulse: 16 (over y, z), tile: 4 (over x), band: 2 (over core).
Axes of the slice: x: 4, y: 4, z: 4, core: 2. Of those that a mesh axis runs over, the one named last changes fastest.
Arguments:
- echo: bfloat16 [2, 16, 16384], P(None, 'pulse', 'band'), may hold values from -6 to 6
- offsets: int32 [16, 32, 4096], P('pulse', 'tile'), may hold values from 0 to 8184
- delta: float32 [16], P('pulse'), may hold values from -3 to 3
- look: float32 [16, 4096], P('pulse'), may hold values from 0.5 to 1.5
Outputs:
- image: float32 [2, 32, 4096], P(None, 'tile', 'pulse')
- focus_gradient: float32 [16], P('pulse')
All inputs are finite; a program needn't handle non-finite values.
Results may differ from a plain program's by a relative error of at most 0.0003.
Values sent between devices are 32-bit elements; how exact they have to be, the bound alone decides.
No kernel may reach another device: no remote copies, remote signals or barrier semaphores. Data moves between devices by JAX's collectives and lax.ppermute only.
A program may use at most 64 MiB of HBM per device.

v0:
```python
import math

import jax
import jax.numpy as jnp
from jax import lax
from jax.sharding import PartitionSpec as P

filter_taps = (-0.0136, 0.0637, -0.1804, 0.6366, 0.6366, -0.1804, 0.0637, -0.0136)
power_floor = 1e-06


def filtered(echo_part):
    length = echo_part.shape[-1] - 7
    summed = filter_taps[0] * echo_part[..., 0:length].astype(jnp.float32)
    for lag_index in range(1, 8):
        summed = summed + filter_taps[lag_index] * echo_part[
            ..., lag_index : lag_index + length
        ].astype(jnp.float32)
    return summed


def lookup_rows(table, indices):
    return table[indices]


def pulse_terms(pairs, offsets, delta, look, multiplier):
    flat = offsets.reshape(offsets.shape[0], -1)
    fetched = jax.vmap(lookup_rows)(pairs, flat)
    real_in = fetched[:, :, 0].reshape(offsets.shape)
    imag_in = fetched[:, :, 1].reshape(offsets.shape)
    phase_index = offsets * multiplier % 64
    angle = (
        phase_index.astype(jnp.float32) * (math.pi / 32.0) + delta[:, None, None] * look[:, None, :]
    )
    cosine = jnp.cos(angle)
    sine = jnp.sin(angle)
    return (cosine * real_in - sine * imag_in, sine * real_in + cosine * imag_in)


def power_sums(field):
    power = field[0] * field[0] + field[1] * field[1]
    return (jnp.sum(power), jnp.sum(power * power))


def weighted(field, mean_power, quart):
    power = field[0] * field[0] + field[1] * field[1]
    weight = 2.0 * power / (mean_power * mean_power) - 2.0 * quart / (
        mean_power * mean_power * mean_power
    )
    return jnp.stack((weight * field[0], weight * field[1]))


def local(echo, offsets, delta, look):
    pulses_dev, rows_dev, columns = offsets.shape
    npix = rows_dev * lax.axis_size("tile") * columns
    pulses_all = pulses_dev * lax.axis_size("pulse")
    multiplier = 5 + 2 * lax.axis_index("band")
    filt = filtered(echo)
    pairs = jnp.stack((filt[0], filt[1]), axis=-1)
    real_t, imag_t = pulse_terms(pairs, offsets, delta, look, multiplier)
    partial_value = jnp.stack((jnp.sum(real_t, axis=0), jnp.sum(imag_t, axis=0)))
    slab = lax.psum_scatter(partial_value, "pulse", scatter_dimension=2, tiled=True)
    image = lax.psum(slab, "band")
    power_total, quart_total = lax.psum(power_sums(image), ("pulse", "tile"))
    mean_power = power_total / npix + power_floor
    quart = quart_total / npix
    adjoint = lax.all_gather(weighted(image, mean_power, quart), "pulse", axis=2, tiled=True)
    mixed = adjoint[1][None] * real_t - adjoint[0][None] * imag_t
    local_grad = jnp.sum(jnp.sum(mixed, axis=1) * look, axis=1)
    summed_grad = lax.psum(local_grad, ("tile", "band"))
    focus_gradient = math.sqrt(pulses_all / npix) * summed_grad
    return (image, focus_gradient)


def solution(mesh):
    in_specs = (P(None, "pulse", "band"), P("pulse", "tile", None), P("pulse"), P("pulse", None))
    out_specs = (P(None, "tile", "pulse"), P("pulse"))
    return jax.shard_map(local, mesh=mesh, in_specs=in_specs, out_specs=out_specs, check_vma=False)
```

profile of v0, /device:TPU:1, one launch (start us, length us, event | category | flops | bytes accessed | tf_op | source)
XLA Modules:
  0.0 813.3 jit_solution(8955216203628743202)
XLA Ops:
  7.2 0.0 reduce-scatter.2.cloned.1.call-start
  7.2 1.4 multiply_add_fusion.1
  8.6 0.1 slice_bitcast_fusion.1
  8.7 0.1 pad_maximum_fusion.1
  8.8 6.4 copy.8
  15.2 1.1 reshape.70
  16.2 0.1 compare_select_fusion
  16.4 0.2 pad_bitcast_fusion
  16.6 0.4 fusion.7
  17.0 472.5 %gather_fusion = f32[32768,2]{1,0:T(8,128)} fusion(f32[1,8185,2]{2,0,1:T(1,128)} %copy.8, s32[32768]{0:T(1024)S(1)} %bitcast.13), kind=kCustom, calls=%fused_computation | custom fusion | bytes 786432 | tf_op jit(solution)/shard_map/vmap()/gather | solution.py:23
  489.5 0.0 copy-start.2
  489.5 0.0 copy-start
  489.5 20.1 %slice_reduce_fusion.1 = (f32[32768]{0:T(1024)S(1)}, f32[32768]{0:T(1024)S(1)}) fusion(f32[1,32768,2]{2,1,0:T(8,128)} %bitcast.14), kind=kLoop, calls=%fused_computation.2 | loop fusion | bytes 524288 | tf_op jit(solution)/shard_map/slice | solution.py:29
  510.3 0.0 copy-done.2
  510.4 0.0 copy-done
  510.4 0.6 multiply_subtract_fusion
  510.9 0.7 pad_maximum_fusion
  511.7 0.0 reduce-scatter.2.cloned.1.call-update
  511.7 73.8 %reduce-scatter.2.cloned.1.call-done = f32[2,8,256]{2,1,0:T(8,128)} async-done(((f32[2,8,4096]{2,1,0:T(8,128)}), f32[2,8,256]{2,1,0:T(8,128)}) %reduce-scatter.2.cloned.1.call-update) | async-done | bytes 16400 | tf_op jit(solution)/shard_map/reduce_scatter | solution.py:62
  585.5 6.1 psum.28
  591.6 0.0 copy-start.1
  591.6 0.7 fusion.11
  592.3 149.3 %all-reduce = (f32[]{:T(128)}, f32[]{:T(128)}) all-reduce(f32[]{:T(128)} %get-tuple-element.5, f32[]{:T(128)} %get-tuple-element.4), channel_id=1, replica_groups=mesh['pulse'=16,'tile'=4,'band'=2] {'pulse','tile'}, use_global_device_ids=true, to_apply=%region_5.6 | all-reduce | flops 2 | bytes 16 | tf_op jit(solution)/shard_map/psum | solution.py:64
  742.8 15.8 %all_gather.3 = f32[2,8,4096]{2,1,0:T(8,128)S(1)} all-gather(f32[2,8,256]{2,1,0:T(8,128)S(1)} %pad_maximum_fusion.2), channel_id=1, replica_groups=mesh['pulse'=16,'tile'=4,'band'=2] {'pulse'}, dimensions={2}, use_global_device_ids=true | all-gather | bytes 278528 | tf_op jit(solution)/shard_map/all_gather | solution.py:67
  758.6 0.1 fusion.5
  758.7 0.6 multiply_reduce_fusion
  759.3 45.4 %psum.31 = f32[1]{0:T(128)} all-reduce(f32[1]{0:T(128)} %bitcast.8), channel_id=1, replica_groups=mesh['pulse'=16,'tile'=4,'band'=2] {'tile','band'}, use_global_device_ids=true, to_apply=%region_8.9 | all-reduce | flops 1 | bytes 8 | tf_op jit(solution)/shard_map/psum | solution.py:70
  805.4 0.0 copy-done.1
  (5 shorter events, 0.1 us)
Async XLA Ops:
  7.2 578.3 %reduce-scatter.2.cloned.1.call-start = ((), (), s32[]{:S(2)}) async-start(), calls=%async_computation.1 | async-start | bytes 278528 | tf_op jit(solution)/shard_map/reduce_scatter | solution.py:62
  489.5 20.9 %copy-start.2 = (f32[1,4096]{1,0:T(1,128)S(1)}, f32[1,4096]{1,0:T(1,128)}, u32[]{:S(2)}) copy-start(f32[1,4096]{1,0:T(1,128)} %param.7) | copy-start | bytes 49156
  489.5 20.9 %copy-start = (s32[1,8,4096]{2,1,0:T(8,128)S(1)}, s32[1,8,4096]{2,1,0:T(8,128)}, u32[]{:S(2)}) copy-start(s32[1,8,4096]{2,1,0:T(8,128)} %param.5) | copy-start | bytes 393220
  591.6 213.8 %copy-start.1 = (f32[2,8,256]{2,1,0:T(8,128)}, f32[2,8,256]{2,1,0:T(8,128)S(1)}, u32[]{:S(2)}) copy-start(f32[2,8,256]{2,1,0:T(8,128)S(1)} %psum.28) | copy-start | bytes 49156
Sparse Core Ops, SparseCore 0:
  511.8 73.6 reduce-scatter.1
where the time goes:
time: 817 us; the launch traced here: 813 us
  local copies, waits for them, and re-layouts  500 us (61%)
  blocking collectives  217 us (27%)
  waiting for transfers between devices  73.8 us (9%)
  between operations  17.8 us (2%)
    gather x2, local copies, waits for them, and re-layouts, lookup_rows(): return table[indices]  473 us
    psum x1, blocking collectives, local(): power_total, quart_total = lax.psum(power_sums(image), ('pulse', 'tile'))  149 us
    reduce_scatter x1, waiting for transfers between devices, local(): lax.psum_scatter(partial_value, 'pulse', scatter_dimension=2, tiled=True)  73.8 us
    psum x1, blocking collectives, local(): summed_grad = lax.psum(local_grad, ('tile', 'band'))  45.4 us
    slice x1, local copies, waits for them, and re-layouts, pulse_terms(): real_in = fetched[:, :, 0].reshape(offsets.shape)  20.1 us
  transfers between devices with their start and end apart: 1, of which 1 were waited for; matrix products, arithmetic and copies ran while one was open for 0% of the time, Pallas kernels for 0%

commit v1 on v0

v1 whole, which is shorter than its diff:
```python
import math

import jax
import jax.numpy as jnp
from jax import lax
from jax.experimental import pallas as pl
from jax.experimental.pallas import tpu as pltpu
from jax.sharding import PartitionSpec as P

filter_taps = (-0.0136, 0.0637, -0.1804, 0.6366, 0.6366, -0.1804, 0.0637, -0.0136)
power_floor = 1e-06

LANES = 128
ROWS_DEV = 8
GROUP = 2


def sine_cosine(angle):
    turns = jnp.floor(angle * (2.0 / math.pi) + 0.5)
    rest = angle - turns * 1.5703125
    rest = rest - turns * 4.837512969970703125e-4
    rest = rest - turns * 7.549789948768648e-8
    square = rest * rest
    sine = rest + rest * square * (
        -1.6666654611e-1 + square * (8.3321608736e-3 + square * -1.9515295891e-4)
    )
    cosine = 1.0 - 0.5 * square + square * square * (
        4.166664568298827e-2 + square * (-1.388731625493765e-3 + square * 2.443315711809948e-5)
    )
    quadrant = turns.astype(jnp.int32) & 3
    swap = (quadrant & 1) == 1
    sine_out = jnp.where(swap, cosine, sine)
    cosine_out = jnp.where(swap, sine, cosine)
    sine_out = jnp.where(quadrant >= 2, -sine_out, sine_out)
    cosine_out = jnp.where((quadrant == 1) | (quadrant == 2), -cosine_out, cosine_out)
    return sine_out, cosine_out


def filtered_rows(echo_rows):
    rows = echo_rows.shape[0]
    lane = lax.broadcasted_iota(jnp.int32, echo_rows.shape, 1)
    inside = filter_taps[0] * echo_rows
    across = jnp.zeros_like(echo_rows)
    for lag in range(1, 8):
        moved = filter_taps[lag] * pltpu.roll(echo_rows, LANES - lag, 1)
        here = lane < LANES - lag
        inside = inside + jnp.where(here, moved, 0.0)
        across = across + jnp.where(here, 0.0, moved)
    return inside + pltpu.roll(across, rows - 1, 0)


def lane_lookup(row, lanes):
    return jnp.take_along_axis(row, lanes, axis=1, mode="promise_in_bounds")


def terms_kernel(delta_ref, echo_ref, offsets_ref, look_ref, out_ref, table_ref, turn_ref):
    table_rows = table_ref.shape[1]
    blocks = out_ref.shape[0]
    multiplier = 5 + 2 * lax.axis_index("band")
    lane = lax.broadcasted_iota(jnp.int32, (1, LANES), 1)
    phase_index = (lane * multiplier) & 63
    sine, cosine = sine_cosine(phase_index.astype(jnp.float32) * (math.pi / 32.0))
    filt = []
    for part in range(2):
        rows = echo_ref[part].astype(jnp.float32).reshape(table_rows, LANES)
        filt.append(filtered_rows(rows))
    table_ref[0] = cosine * filt[0] - sine * filt[1]
    table_ref[1] = sine * filt[0] + cosine * filt[1]
    turn_sine, turn_cosine = sine_cosine(delta_ref[0] * look_ref[...])
    turn_ref[0] = turn_cosine
    turn_ref[1] = turn_sine

    def some_blocks(step, carry):
        starts = [pl.multiple_of((step * GROUP + j) * LANES, LANES) for j in range(GROUP)]
        offsets = [offsets_ref[0, :, pl.ds(start, LANES)] for start in starts]
        lanes = [k & (LANES - 1) for k in offsets]
        highs = [k >> 7 for k in offsets]
        bits = [[((high >> bit) & 1) == 1 for bit in range(6)] for high in highs]

        def select(first, level, part):
            if level == 0:
                row = jnp.broadcast_to(table_ref[part, pl.ds(first, 1), :], (ROWS_DEV, LANES))
                return [lane_lookup(row, lanes[j]) for j in range(GROUP)]
            low = select(first, level - 1, part)
            high = select(first + (1 << (level - 1)), level - 1, part)
            return [jnp.where(bits[j][level - 1], high[j], low[j]) for j in range(GROUP)]

        real_in = select(0, 6, 0)
        imag_in = select(0, 6, 1)
        for j in range(GROUP):
            cos_turn = turn_ref[0, :, pl.ds(starts[j], LANES)]
            sin_turn = turn_ref[1, :, pl.ds(starts[j], LANES)]
            out_ref[step * GROUP + j, 0] = cos_turn * real_in[j] - sin_turn * imag_in[j]
            out_ref[step * GROUP + j, 1] = sin_turn * real_in[j] + cos_turn * imag_in[j]
        return carry

    lax.fori_loop(0, blocks // GROUP, some_blocks, 0)


def image_kernel(terms_ref, image_ref, sums_ref):
    pulses = terms_ref.shape[0] // 2
    copies = sums_ref.shape[0] // pulses
    real_parts = []
    imag_parts = []
    for pulse in range(pulses):
        real_parts.append(terms_ref[2 * pulse, 0] + terms_ref[2 * pulse + 1, 0])
        imag_parts.append(terms_ref[2 * pulse, 1] + terms_ref[2 * pulse + 1, 1])
    real = sum(real_parts[1:], real_parts[0])
    imag = sum(imag_parts[1:], imag_parts[0])
    image_ref[0] = real
    image_ref[1] = imag
    power = real * real + imag * imag
    power_row = jnp.sum(power, axis=0, keepdims=True)
    quart_row = jnp.sum(power * power, axis=0, keepdims=True)
    for pulse in range(pulses):
        cross = imag * real_parts[pulse] - real * imag_parts[pulse]
        cross_row = jnp.sum(cross, axis=0, keepdims=True)
        power_cross_row = jnp.sum(power * cross, axis=0, keepdims=True)
        rows = jnp.concatenate((power_cross_row, cross_row, power_row, quart_row), axis=0)
        for copy in range(copies):
            sums_ref[pulse * copies + copy] = rows


def gradient_kernel(own_ref, other_ref, sums_ref, look_ref, image_ref, gradient_ref, *, pulses, npix):
    band = lax.axis_index("band")
    first = jnp.where(band == 0, own_ref[...], other_ref[...])
    second = jnp.where(band == 0, other_ref[...], own_ref[...])
    image_ref[:, :, 0:LANES] = first
    image_ref[:, :, LANES:] = second
    blocks = look_ref.shape[1] // LANES
    tiles = sums_ref.shape[0] // blocks
    weighted = jnp.zeros((4, LANES), jnp.float32)
    for block in range(blocks):
        slab, half = block // 2, block % 2
        found = sums_ref[(slab * tiles) * 2 + half]
        for tile in range(1, tiles):
            found = found + sums_ref[(slab * tiles + tile) * 2 + half]
        row = lax.broadcasted_iota(jnp.int32, (4, LANES), 0)
        look = jnp.broadcast_to(look_ref[:, block * LANES : (block + 1) * LANES], (4, LANES))
        weighted = weighted + found * jnp.where(row < 2, look, 1.0)
    totals = jnp.sum(weighted, axis=1, keepdims=True)
    mean_power = totals[2:3] / npix + power_floor
    quart = totals[3:4] / npix
    gradient = 2.0 * totals[0:1] / (mean_power * mean_power) - 2.0 * quart * totals[1:2] / (
        mean_power * mean_power * mean_power
    )
    gradient_ref[...] = jnp.broadcast_to(math.sqrt(pulses / npix) * gradient, gradient_ref.shape)


def vmem(count):
    return [pl.BlockSpec(memory_space=pltpu.VMEM)] * count


def local(echo, offsets, delta, look):
    pulses_dev, rows_dev, columns = offsets.shape
    bins = echo.shape[2]
    blocks = columns // LANES
    tiles = lax.axis_size("tile")
    pulses = lax.axis_size("pulse")
    bands = lax.axis_size("band")
    npix = rows_dev * tiles * columns
    terms = pl.pallas_call(
        terms_kernel,
        out_shape=jax.ShapeDtypeStruct((blocks, 2, rows_dev, LANES), jnp.float32),
        in_specs=[pl.BlockSpec(memory_space=pltpu.SMEM)] + vmem(3),
        out_specs=pl.BlockSpec(memory_space=pltpu.VMEM),
        scratch_shapes=[
            pltpu.VMEM((2, bins // LANES, LANES), jnp.float32),
            pltpu.VMEM((2, 1, columns), jnp.float32),
        ],
        name="terms",
    )(delta, echo, offsets, look)
    terms = lax.all_to_all(terms, ("pulse", "band"), 0, 0, tiled=True)
    half, sums = pl.pallas_call(
        image_kernel,
        out_shape=(
            jax.ShapeDtypeStruct((2, rows_dev, LANES), jnp.float32),
            jax.ShapeDtypeStruct((pulses * tiles * bands, 4, LANES), jnp.float32),
        ),
        in_specs=vmem(1),
        out_specs=vmem(2),
        name="image_sums",
    )(terms)
    other = lax.ppermute(half, "band", [(0, 1), (1, 0)])
    sums = lax.all_to_all(sums, ("pulse", "tile", "band"), 0, 0, tiled=True)
    image, gradient = pl.pallas_call(
        lambda *refs: gradient_kernel(*refs, pulses=pulses, npix=npix),
        out_shape=(
            jax.ShapeDtypeStruct((2, rows_dev, 2 * LANES), jnp.float32),
            jax.ShapeDtypeStruct((1, LANES), jnp.float32),
        ),
        in_specs=vmem(4),
        out_specs=vmem(2),
        name="gradient",
    )(half, other, sums, look)
    return image, gradient[0, 0:1]


def solution(mesh):
    in_specs = (P(None, "pulse", "band"), P("pulse", "tile", None), P("pulse"), P("pulse", None))
    out_specs = (P(None, "tile", "pulse"), P("pulse"))
    return jax.shard_map(local, mesh=mesh, in_specs=in_specs, out_specs=out_specs, check_vma=False)
```

time: 817 us -> 49.9 us (0.06)
  local copies, waits for them, and re-layouts: 500 us -> 2.13 us
  blocking collectives: 217 us -> 18.7 us
  waiting for transfers between devices: 73.8 us -> 9.76 us
  between operations: 17.8 us -> 1.3 us
  Pallas kernels: 0 us -> 10.9 us
    gather x2 -> x0, local copies, waits for them, and re-layouts: 473 us -> none  [lookup_rows(): return table[indices]]
    psum x3 -> x0, blocking collectives: 201 us -> none  [the longest x1 149 us: local(): power_total, quart_total = lax.psum(power_sums(image), ('pulse', 'tile'))]
    reduce_scatter x1 -> x0, waiting for transfers between devices: 73.8 us -> none  [local(): lax.psum_scatter(partial_value, 'pulse', scatter_dimension=2, tiled=True)]
    slice x1 -> x0, local copies, waits for them, and re-layouts: 20.1 us -> none  [pulse_terms(): real_in = fetched[:, :, 0].reshape(offsets.shape)]
    all_to_all x0 -> x1, blocking collectives: none -> 18.7 us  [local(): terms = lax.all_to_all(terms, ('pulse', 'band'), 0, 0, tiled=True)]
    all_gather x1 -> x0, blocking collectives: 15.8 us -> none  [local(): lax.all_gather(weighted(image, mean_power, quart), 'pulse', axis=2, tiled...]
    pallas_call x0 -> x3, Pallas kernels: none -> 10.9 us  [the longest x1 7.48 us: local(): pl.pallas_call(terms_kernel, out_shape=jax.ShapeDtypeStruct((blocks, 2, r...]
    all_to_all x0 -> x1, waiting for transfers between devices: none -> 8.93 us  [local(): sums = lax.all_to_all(sums, ('pulse', 'tile', 'band'), 0, 0, tiled=True)]
  transfers between devices with their start and end apart: 1 -> 2, of which waited for: 1 -> 2; matrix products, arithmetic and copies ran while one was open for 0% -> 0% of each run, Pallas kernels for 0% -> 0%
where the time goes in v1:
time: 49.9 us; the launch traced here: 49.5 us
  blocking collectives  18.7 us (37%)
  Pallas kernels  10.9 us (22%)
  waiting for transfers between devices  9.76 us (20%)
  starting transfers between devices  6.71 us (13%)
  local copies, waits for them, and re-layouts  2.13 us (4%)
  between operations  1.3 us (3%)
    all_to_all x1, blocking collectives, local(): terms = lax.all_to_all(terms, ('pulse', 'band'), 0, 0, tiled=True)  18.7 us
    all_to_all x1, waiting for transfers between devices, local(): sums = lax.all_to_all(sums, ('pulse', 'tile', 'band'), 0, 0, tiled=True)  8.93 us
    pallas_call x1, Pallas kernels, local(): pl.pallas_call(terms_kernel, out_shape=jax.ShapeDtypeStruct((blocks, 2, r...  7.48 us
    all_to_all x1, starting transfers between devices, local(): sums = lax.all_to_all(sums, ('pulse', 'tile', 'band'), 0, 0, tiled=True)  5.56 us
    unnamed x7, local copies, waits for them, and re-layouts  2.13 us
    pallas_call x1, Pallas kernels, local(): pl.pallas_call(image_kernel, out_shape=(jax.ShapeDtypeStruct((2, rows_dev...  1.73 us
    pallas_call x1, Pallas kernels, local(): pl.pallas_call(lambda *refs: gradient_kernel(*refs, pulses=pulses, npix=n...  1.7 us
    ppermute x1, starting transfers between devices, local(): other = lax.ppermute(half, 'band', [(0, 1), (1, 0)])  1.15 us
  transfers between devices with their start and end apart: 2, of which 2 were waited for; matrix products, arithmetic and copies ran while one was open for 0% of the time, Pallas kernels for 0%

profile of v1, /device:TPU:1, one launch (start us, length us, event | category | flops | bytes accessed | tf_op | source)
XLA Modules:
  0.0 49.5 jit_solution(141206897707565315)
XLA Ops:
  1.3 1.4 %copy.6.echo_ref = bf16[2,1,8192]{2,1,0:T(2,128)(2,1)} copy(bf16[2,1,8192]{2,0,1:T(2,128)(2,1)} %param.4) | data formatting | bytes 65536 | tf_op args[0]
  2.7 7.5 %terms.1 = f32[32,2,8,128]{3,2,1,0:T(8,128)} custom-call(f32[1]{0:T(128)S(6)} %copy.7.delta_ref, bf16[2,1,8192]{2,1,0:T(2,128)(2,1)} %copy.6.echo_ref, s32[1,8,4096]{2,1,0:T(8,128)} %offsets_ref.1, f32[1,4096]{1,0:T(1,128)} %refs_3_.1), custom_call_target="tpu_custom_call" | custom-call | tf_op jit(solution)/shard_map/terms/pallas_call | solution.py:162
  10.2 18.7 %all_to_all.10.terms_ref = f32[32,2,8,128]{3,2,1,0:T(8,128)} all-to-all(f32[32,2,8,128]{3,2,1,0:T(8,128)} %terms.1), channel_id=1, replica_groups=mesh['pulse'=16,'tile'=4,'band'=2] {'pulse','band'}, dimensions={0} | all-to-all | bytes 524288 | tf_op jit(solution)/shard_map/all_to_all | solution.py:173
  28.9 1.7 %image_sums.1 = (f32[2,8,128]{2,1,0:T(8,128)}, f32[128,4,128]{2,1,0:T(4,128)}) custom-call(f32[32,2,8,128]{3,2,1,0:T(8,128)} %all_to_all.10.terms_ref), custom_call_target="tpu_custom_call" | custom-call | tf_op jit(solution)/shard_map/image_sums/pallas_call | solution.py:174
  30.6 0.0 copy-start.1
  30.6 5.6 %all-to-all-start.1 = ((f32[128,4,128]{2,1,0:T(4,128)}), f32[128,4,128]{2,1,0:T(4,128)S(1)}, u32[]{:S(2)}, u32[]{:S(2)}) async-start(f32[128,4,128]{2,1,0:T(4,128)} %get-tuple-element.7), calls=%async_computation.1 | async-start | bytes 524288 | tf_op jit(solution)/shard_map/all_to_all | solution.py:185
  36.2 0.0 copy-done.1
  36.2 1.1 %collective-permute-start = (f32[2,8,128]{2,1,0:T(8,128)S(1)}, f32[2,8,128]{2,1,0:T(8,128)S(1)}, u32[]{:S(2)}, u32[]{:S(2)}) collective-permute-start(f32[2,8,128]{2,1,0:T(8,128)S(1)} %copy-done.1), channel_id=1, source_target_pairs={{0,1},{1,0},{2,3},{3,2},{4,5},{5,4},{6,7},{7,6},{8,9},{9,8},{10,11... | collective-permute-start | bytes 24584 | tf_op jit(solution)/shard_map/ppermute | solution.py:184
  37.3 0.8 %collective-permute-done.refs_1_ = f32[2,8,128]{2,1,0:T(8,128)S(1)} collective-permute-done((f32[2,8,128]{2,1,0:T(8,128)S(1)}, f32[2,8,128]{2,1,0:T(8,128)S(1)}, u32[]{:S(2)}, u32[]{:S(2)}) %collective-permute-start) | collective-permute-done | bytes 8224 | tf_op jit(solution)/shard_map/ppermute | solution.py:184
  38.2 0.0 copy-start.2
  38.2 8.9 %all-to-all-done.1.refs_2_ = f32[128,4,128]{2,1,0:T(4,128)S(1)} async-done(((f32[128,4,128]{2,1,0:T(4,128)}), f32[128,4,128]{2,1,0:T(4,128)S(1)}, u32[]{:S(2)}, u32[]{:S(2)}) %all-to-all-start.1) | async-done | bytes 262176 | tf_op jit(solution)/shard_map/all_to_all | solution.py:185
  47.1 0.0 copy-done.2
  47.1 0.0 copy-start
  47.1 0.7 %copy-done = f32[128,4,128]{2,1,0:T(4,128)} copy-done((f32[128,4,128]{2,1,0:T(4,128)}, f32[128,4,128]{2,1,0:T(4,128)S(1)}, u32[]{:S(2)}) %copy-start) | copy-done | bytes 262168
  47.8 1.7 %gradient.1 = (f32[2,8,256]{2,1,0:T(8,128)}, f32[1,128]{1,0:T(1,128)}) custom-call(f32[2,8,128]{2,1,0:T(8,128)} %get-tuple-element.6.refs_0_, f32[2,8,128]{2,1,0:T(8,128)} %copy-done.2, f32[128,4,128]{2,1,0:T(4,128)} %copy-done, f32[1,4096]{1,0:T(1,128)} %refs_3_.1), custom_call_target="tpu_custom_call" | custom-call | tf_op jit(solution)/shard_map/gradient/pallas_call | solution.py:186
Async XLA Ops:
  30.6 5.6 %copy-start.1 = (f32[2,8,128]{2,1,0:T(8,128)S(1)}, f32[2,8,128]{2,1,0:T(8,128)}, u32[]{:S(2)}) copy-start(f32[2,8,128]{2,1,0:T(8,128)} %get-tuple-element.6.refs_0_) | copy-start | bytes 24580
  30.6 16.5 %all-to-all-start.1 = ((f32[128,4,128]{2,1,0:T(4,128)}), f32[128,4,128]{2,1,0:T(4,128)S(1)}, u32[]{:S(2)}, u32[]{:S(2)}) async-start(f32[128,4,128]{2,1,0:T(4,128)} %get-tuple-element.7), calls=%async_computation.1 | async-start | bytes 524288 | tf_op jit(solution)/shard_map/all_to_all | solution.py:185
  36.2 2.0 %collective-permute-start = (f32[2,8,128]{2,1,0:T(8,128)S(1)}, f32[2,8,128]{2,1,0:T(8,128)S(1)}, u32[]{:S(2)}, u32[]{:S(2)}) collective-permute-start(f32[2,8,128]{2,1,0:T(8,128)S(1)} %copy-done.1), channel_id=1, source_target_pairs={{0,1},{1,0},{2,3},{3,2},{4,5},{5,4},{6,7},{7,6},{8,9},{9,8},{10,11... | collective-permute-start | bytes 24584 | tf_op jit(solution)/shard_map/ppermute | solution.py:184
  38.2 8.9 %copy-start.2 = (f32[2,8,128]{2,1,0:T(8,128)}, f32[2,8,128]{2,1,0:T(8,128)S(1)}, u32[]{:S(2)}) copy-start(f32[2,8,128]{2,1,0:T(8,128)S(1)} %collective-permute-done.refs_1_) | copy-start | bytes 24580
  47.1 0.7 %copy-start = (f32[128,4,128]{2,1,0:T(4,128)}, f32[128,4,128]{2,1,0:T(4,128)S(1)}, u32[]{:S(2)}) copy-start(f32[128,4,128]{2,1,0:T(4,128)S(1)} %all-to-all-done.1.refs_2_) | copy-start | bytes 786436

commit v2 on v1

v2 whole, which is shorter than its diff:
```python
import math

import jax
import jax.numpy as jnp
from jax import lax
from jax.experimental import pallas as pl
from jax.experimental.pallas import tpu as pltpu
from jax.sharding import PartitionSpec as P

filter_taps = (-0.0136, 0.0637, -0.1804, 0.6366, 0.6366, -0.1804, 0.0637, -0.0136)
power_floor = 1e-06

LANES = 128
ROWS_DEV = 8
GROUP = 4
CHUNK = 2 * ROWS_DEV + 1
MOST = 8191.0
STEPS = 15
VMEM_BYTES = 8 * 1024 * 1024


def sine_cosine(angle):
    turns = jnp.floor(angle * (2.0 / math.pi) + 0.5)
    rest = angle - turns * 1.5703125
    rest = rest - turns * 4.837512969970703125e-4
    rest = rest - turns * 7.549789948768648e-8
    square = rest * rest
    sine = rest + rest * square * (
        -1.6666654611e-1 + square * (8.3321608736e-3 + square * -1.9515295891e-4)
    )
    cosine = 1.0 - 0.5 * square + square * square * (
        4.166664568298827e-2 + square * (-1.388731625493765e-3 + square * 2.443315711809948e-5)
    )
    quadrant = turns.astype(jnp.int32) & 3
    swap = (quadrant & 1) == 1
    sine_out = jnp.where(swap, cosine, sine)
    cosine_out = jnp.where(swap, sine, cosine)
    sine_out = jnp.where(quadrant >= 2, -sine_out, sine_out)
    cosine_out = jnp.where((quadrant == 1) | (quadrant == 2), -cosine_out, cosine_out)
    return sine_out, cosine_out


def filtered_rows(echo_rows):
    rows = echo_rows.shape[0]
    lane = lax.broadcasted_iota(jnp.int32, echo_rows.shape, 1)
    inside = filter_taps[0] * echo_rows
    across = jnp.zeros_like(echo_rows)
    for lag in range(1, 8):
        moved = filter_taps[lag] * pltpu.roll(echo_rows, LANES - lag, 1)
        here = lane < LANES - lag
        inside = inside + jnp.where(here, moved, 0.0)
        across = across + jnp.where(here, 0.0, moved)
    return inside + pltpu.roll(across, rows - 1, 0)


def lane_lookup(row, lanes):
    return jnp.take_along_axis(row, lanes, axis=1, mode="promise_in_bounds")


def table_kernel(
    delta_hbm, echo_hbm, offsets_hbm, look_hbm, table_ref, offsets_ref, look_ref, angle_ref, echo_ref, delta_ref, arrived
):
    band = lax.axis_index("band")
    slabs = offsets_ref.shape[0]
    copies = [pltpu.make_async_copy(echo_hbm, echo_ref, arrived.at[0])]
    copies.append(pltpu.make_async_copy(look_hbm, look_ref, arrived.at[1]))
    copies.append(pltpu.make_async_copy(delta_hbm, delta_ref, arrived.at[2]))
    for slab in range(slabs):
        start = pl.multiple_of((2 * slab + band) * LANES, LANES)
        copies.append(
            pltpu.make_async_copy(
                offsets_hbm.at[0, :, pl.ds(start, LANES)], offsets_ref.at[slab], arrived.at[3 + slab]
            )
        )
    for copy in copies:
        copy.start()
    lane = lax.broadcasted_iota(jnp.int32, (1, LANES), 1)
    phase_index = (lane * (5 + 2 * band)) & 63
    sine, cosine = sine_cosine(phase_index.astype(jnp.float32) * (math.pi / 32.0))
    copies[0].wait()
    filt = []
    for part in range(2):
        rows = echo_ref[part : part + 1].astype(jnp.float32).reshape(table_ref.shape[1], LANES)
        filt.append(filtered_rows(rows))
    table_ref[0] = cosine * filt[0] - sine * filt[1]
    table_ref[1] = sine * filt[0] + cosine * filt[1]
    copies[1].wait()
    copies[2].wait()
    angle_ref[...] = delta_ref[...] * look_ref[...]
    for copy in copies[3:]:
        copy.wait()


def pack(table_ref, words_ref):
    real, imag = table_ref[0], table_ref[1]
    size = jnp.maximum(jnp.abs(real), jnp.abs(imag))
    top = jnp.max(jnp.max(size, axis=0, keepdims=True), axis=1, keepdims=True)
    top = jnp.where(top > 0.0, top, 1.0)
    shrink = 1.0 / top
    size = size * shrink
    power = jnp.zeros(size.shape, jnp.int32)
    for step in range(1, STEPS + 1):
        power = power + jnp.where(size > 2.0**-step, 1, 0)
    grow = (1 << (STEPS - power)).astype(jnp.float32) * MOST
    real = jnp.floor(real * shrink * grow + 0.5).astype(jnp.int32)
    imag = jnp.floor(imag * shrink * grow + 0.5).astype(jnp.int32)
    words_ref[...] = (real << 18) | ((imag & 0x3FFF) << 4) | power
    return top


def unpack(word):
    unit = (1 << (word & 15)).astype(jnp.float32) * (1.0 / (MOST * 2.0**STEPS))
    return (word >> 18).astype(jnp.float32) * unit, ((word << 14) >> 18).astype(jnp.float32) * unit


def look_up(words_ref, offsets):
    lanes = offsets & (LANES - 1)
    high = offsets >> 7
    found = None
    for row in range(words_ref.shape[0]):
        spread = jnp.broadcast_to(words_ref[pl.ds(row, 1), :], offsets.shape)
        here = lane_lookup(spread, lanes)
        found = here if row == 0 else jnp.where(high == row, here, found)
    return found


def own_kernel(table_ref, offsets_ref, angle_ref, out_ref, turn_ref, words_ref):
    slabs = out_ref.shape[0]
    band = lax.axis_index("band")
    top = pack(table_ref, words_ref)

    def some_blocks(step, carry):
        for j in range(GROUP):
            slab = step * GROUP + j
            real, imag = unpack(look_up(words_ref, offsets_ref[slab]))
            out_ref[slab, 0] = top * real
            out_ref[slab, 1] = top * imag
            start = pl.multiple_of((2 * slab + band) * LANES, LANES)
            sine, cosine = sine_cosine(angle_ref[:, pl.ds(start, LANES)])
            turn_ref[slab, 0:1] = cosine
            turn_ref[slab, 1:2] = sine
        return carry

    lax.fori_loop(0, slabs // GROUP, some_blocks, 0)


def other_kernel(table_ref, offsets_ref, look_ref, own_ref, turn_ref, out_ref, words_ref):
    slabs = own_ref.shape[0]
    band = lax.axis_index("band")
    top = pack(table_ref, words_ref)

    def some_blocks(step, carry):
        for j in range(GROUP):
            slab = step * GROUP + j
            real, imag = unpack(look_up(words_ref, offsets_ref[slab]))
            real = own_ref[slab, 0] + top * real
            imag = own_ref[slab, 1] + top * imag
            cosine = turn_ref[slab, 0:1]
            sine = turn_ref[slab, 1:2]
            first = slab * CHUNK
            out_ref[pl.ds(first, ROWS_DEV), 0, :] = cosine * real - sine * imag
            out_ref[pl.ds(first + ROWS_DEV, ROWS_DEV), 0, :] = sine * real + cosine * imag
            start = pl.multiple_of((2 * slab + band) * LANES, LANES)
            out_ref[first + 2 * ROWS_DEV] = look_ref[:, pl.ds(start, LANES)]
        return carry

    lax.fori_loop(0, slabs // GROUP, some_blocks, 0)


def image_kernel(terms_ref, image_ref, sums_ref):
    pulses = terms_ref.shape[0] // CHUNK
    copies = sums_ref.shape[0] // pulses
    reals = [terms_ref[p * CHUNK : p * CHUNK + ROWS_DEV, 0, :] for p in range(pulses)]
    imags = [terms_ref[p * CHUNK + ROWS_DEV : p * CHUNK + 2 * ROWS_DEV, 0, :] for p in range(pulses)]
    looks = [terms_ref[p * CHUNK + 2 * ROWS_DEV] for p in range(pulses)]
    real = sum(reals[1:], reals[0])
    imag = sum(imags[1:], imags[0])
    image_ref[0] = real
    image_ref[1] = imag
    power = real * real + imag * imag
    power_sum = jnp.sum(jnp.sum(power, axis=0, keepdims=True), axis=1, keepdims=True)
    quart_sum = jnp.sum(jnp.sum(power * power, axis=0, keepdims=True), axis=1, keepdims=True)
    cross_rows, power_cross_rows = [], []
    for p in range(pulses):
        cross = imag * reals[p] - real * imags[p]
        cross_rows.append(looks[p] * jnp.sum(cross, axis=0, keepdims=True))
        power_cross_rows.append(looks[p] * jnp.sum(power * cross, axis=0, keepdims=True))
    cross_sums = jnp.sum(jnp.concatenate(cross_rows, axis=0), axis=1, keepdims=True)
    power_cross_sums = jnp.sum(jnp.concatenate(power_cross_rows, axis=0), axis=1, keepdims=True)
    lane = lax.broadcasted_iota(jnp.int32, (pulses, LANES), 1)
    sums = jnp.where(lane == 0, power_cross_sums, 0.0) + jnp.where(lane == 1, cross_sums, 0.0)
    sums = sums + jnp.where(lane == 2, power_sum, 0.0) + jnp.where(lane == 3, quart_sum, 0.0)
    for p in range(pulses):
        sums_ref[p * copies : (p + 1) * copies, 0, :] = jnp.broadcast_to(sums[p : p + 1], (copies, LANES))


def join_kernel(own_ref, other_ref, image_ref):
    band = lax.axis_index("band")
    image_ref[:, :, 0:LANES] = jnp.where(band == 0, own_ref[...], other_ref[...])
    image_ref[:, :, LANES:] = jnp.where(band == 0, other_ref[...], own_ref[...])


def gradient_kernel(sums_ref, gradient_ref, *, pulses, npix):
    totals = jnp.sum(sums_ref[:, 0, :], axis=0, keepdims=True)
    mean_power = totals[:, 2:3] / npix + power_floor
    quart = totals[:, 3:4] / npix
    gradient = 2.0 * totals[:, 0:1] / (mean_power * mean_power) - 2.0 * quart * totals[:, 1:2] / (
        mean_power * mean_power * mean_power
    )
    gradient_ref[...] = jnp.broadcast_to(math.sqrt(pulses / npix) * gradient, gradient_ref.shape)


SMEM, VMEM, HBM = (pl.BlockSpec(memory_space=space) for space in (pltpu.SMEM, pltpu.VMEM, pltpu.HBM))


def on_device(kernel, out, *operands, name, spaces=None, scratch=(), flops=0):
    return pl.pallas_call(
        kernel,
        out_shape=tuple(jax.ShapeDtypeStruct(shape, dtype) for shape, dtype in out),
        in_specs=spaces or [VMEM] * len(operands),
        out_specs=(VMEM,) * len(out),
        scratch_shapes=scratch,
        compiler_params=pltpu.CompilerParams(vmem_limit_bytes=VMEM_BYTES),
        cost_estimate=pl.CostEstimate(flops=flops, bytes_accessed=1 << 20, transcendentals=0),
        name=name,
    )(*operands)


def local(echo, offsets, delta, look):
    rows_dev, columns = offsets.shape[1:]
    bins = echo.shape[2]
    tiles = lax.axis_size("tile")
    pulses = lax.axis_size("pulse")
    bands = lax.axis_size("band")
    slabs = columns // (LANES * bands)
    npix = rows_dev * tiles * columns
    swap = [(0, 1), (1, 0)]
    f32, i32 = jnp.float32, jnp.int32
    table_shape = (2, bins // LANES, LANES)
    words = pltpu.VMEM(table_shape[1:], i32)
    half_shape = (2, rows_dev, LANES)

    inputs = (delta.reshape(1, 1), echo.reshape(2, bins), offsets, look)
    table, own_offsets, look, angle = on_device(
        table_kernel,
        [(table_shape, f32), ((slabs, rows_dev, LANES), i32), ((1, columns), f32), ((1, columns), f32)],
        inputs[0], *(pltpu.with_memory_space_constraint(array, pltpu.HBM) for array in inputs[1:]),
        name="table", spaces=[pl.BlockSpec(memory_space=pl.ANY)] + [HBM] * 3,
        scratch=[
            pltpu.VMEM((2, bins), echo.dtype),
            pltpu.VMEM((1, 1), f32),
            pltpu.SemaphoreType.DMA((3 + slabs,)),
        ],
    )
    other_table = lax.ppermute(table, "band", swap)
    own, turn = on_device(
        own_kernel,
        [((slabs,) + half_shape, f32), ((slabs, 2, LANES), f32)],
        table, own_offsets, angle,
        name="own_lookup", scratch=[words], flops=1 << 30,
    )
    (terms,) = on_device(
        other_kernel,
        [((slabs * CHUNK, 1, LANES), f32)],
        other_table, own_offsets, look, own, turn,
        name="other_lookup", scratch=[words],
    )
    terms = lax.all_to_all(terms, "pulse", 0, 0, tiled=True)
    half, sums = on_device(
        image_kernel, [(half_shape, f32), ((pulses * tiles * bands, 1, LANES), f32)], terms, name="image_sums"
    )
    other_half = lax.ppermute(half, "band", swap)
    sums = lax.all_to_all(sums, ("pulse", "tile", "band"), 0, 0, tiled=True)
    (image,) = on_device(join_kernel, [((2, rows_dev, 2 * LANES), f32)], half, other_half, name="join")
    (gradient,) = on_device(
        lambda *refs: gradient_kernel(*refs, pulses=pulses, npix=npix), [((1, LANES), f32)], sums, name="gradient"
    )
    return image, gradient[0, 0:1]


def solution(mesh):
    in_specs = (P(None, "pulse", "band"), P("pulse", "tile", None), P("pulse"), P("pulse", None))
    out_specs = (P(None, "tile", "pulse"), P("pulse"))
    return jax.shard_map(local, mesh=mesh, in_specs=in_specs, out_specs=out_specs, check_vma=False)
```

time: 49.9 us -> 40.1 us (0.80)
  blocking collectives: 18.7 us -> 14.5 us
  Pallas kernels: 10.9 us -> 6.81 us
  starting transfers between devices: 6.71 us -> 9.57 us
  local copies, waits for them, and re-layouts: 2.13 us -> 0 us
  waiting for transfers between devices: 9.76 us -> 7.74 us
    all_to_all x1, blocking collectives: 18.7 us -> 14.5 us  [local(): terms = lax.all_to_all(terms, 'pulse', 0, 0, tiled=True)]
    pallas_call x3 -> x6, Pallas kernels: 10.9 us -> 6.81 us  [on_device(): pl.pallas_call(kernel, out_shape=tuple((jax.ShapeDtypeStruct(shape, dtype...]
    unnamed x7 -> x0, local copies, waits for them, and re-layouts: 2.13 us -> none
    all_to_all x1, waiting for transfers between devices: 8.93 us -> 6.91 us  [local(): sums = lax.all_to_all(sums, ('pulse', 'tile', 'band'), 0, 0, tiled=True)]
    ppermute x1 -> x2, starting transfers between devices: 1.15 us -> 2.65 us  [the longest x1 1.5 us: local(): other_table = lax.ppermute(table, 'band', swap)]
    all_to_all x1, starting transfers between devices: 5.56 us -> 6.92 us  [local(): sums = lax.all_to_all(sums, ('pulse', 'tile', 'band'), 0, 0, tiled=True)]
  transfers between devices with their start and end apart: 2 -> 3, of which waited for: 2 -> 2; matrix products, arithmetic and copies ran while one was open for 0% -> 0% of each run, Pallas kernels for 0% -> 6%
where the time goes in v2:
time: 40.1 us; the launch traced here: 39.9 us
  blocking collectives  14.5 us (36%)
  starting transfers between devices  9.57 us (24%)
  waiting for transfers between devices  7.74 us (19%)
  Pallas kernels  6.81 us (17%)
  between operations  1.31 us (3%)
    all_to_all x1, blocking collectives, local(): terms = lax.all_to_all(terms, 'pulse', 0, 0, tiled=True)  14.5 us
    all_to_all x1, starting transfers between devices, local(): sums = lax.all_to_all(sums, ('pulse', 'tile', 'band'), 0, 0, tiled=True)  6.92 us
    all_to_all x1, waiting for transfers between devices, local(): sums = lax.all_to_all(sums, ('pulse', 'tile', 'band'), 0, 0, tiled=True)  6.91 us
    pallas_call x6, Pallas kernels, on_device(): pl.pallas_call(kernel, out_shape=tuple((jax.ShapeDtypeStruct(shape, dtype...  6.81 us
    ppermute x1, starting transfers between devices, local(): other_table = lax.ppermute(table, 'band', swap)  1.5 us
    ppermute x1, starting transfers between devices, local(): other_half = lax.ppermute(half, 'band', swap)  1.15 us
    ppermute x1, waiting for transfers between devices, local(): other_half = lax.ppermute(half, 'band', swap)  0.83 us
  transfers between devices with their start and end apart: 3, of which 2 were waited for; matrix products, arithmetic and copies ran while one was open for 0% of the time, Pallas kernels for 6%

profile of v2, /device:TPU:1, one launch (start us, length us, event | category | flops | bytes accessed | tf_op | source)
XLA Modules:
  0.0 39.9 jit_solution(10522314861609716403)
XLA Ops:
  1.3 1.2 %table.1 = (f32[2,64,128]{2,1,0:T(8,128)S(1)}, s32[16,8,128]{2,1,0:T(8,128)S(1)}, f32[1,4096]{1,0:T(1,128)S(1)}, f32[1,4096]{1,0:T(1,128)S(1)}) custom-call(f32[1,1]{1,0:T(1,128)} %bitcast.4.delta_hbm, bf16[2,8192]{1,0:T(2,128)(2,1)} %bitcast.5, s32[1,8,4096]{2,1,0:T(8,128)} %offsets_hbm.1, f32[1,4096]{1,0:T(1,128)} %look_hbm.1), custom_call_target="tpu_custom_call" | custom-call | bytes 1048576 | tf_op jit(solution)/shard_map/table/pallas_call | solution.py:217
  2.5 1.5 %collective-permute-start = (f32[2,64,128]{2,1,0:T(8,128)S(1)}, f32[2,64,128]{2,1,0:T(8,128)S(1)}, u32[]{:S(2)}, u32[]{:S(2)}) collective-permute-start(f32[2,64,128]{2,1,0:T(8,128)S(1)} %get-tuple-element.10.table_ref), channel_id=1, source_target_pairs={{0,1},{1,0},{2,3},{3,2},{4,5},{5,4},{6,7},{7,6},{8,9},{9,8},{10,11... | collective-permute-start | bytes 196616 | tf_op jit(solution)/shard_map/ppermute | solution.py:255
  4.0 1.6 %own_lookup.1 = (f32[16,2,8,128]{3,2,1,0:T(8,128)S(1)}, f32[16,2,128]{2,1,0:T(2,128)S(1)}) custom-call(f32[2,64,128]{2,1,0:T(8,128)S(1)} %get-tuple-element.10.table_ref, s32[16,8,128]{2,1,0:T(8,128)S(1)} %get-tuple-element.11.offsets_ref, f32[1,4096]{1,0:T(1,128)S(1)} %get-tuple-element.13.angle_ref), custom_call_target="tpu_custom_call" | custom-call | flops 1073741824 | bytes 1048576 | tf_op jit(solution)/shard_map/own_lookup/pallas_call | solution.py:217
  5.6 0.0 collective-permute-done.table_ref
  5.6 1.6 %other_lookup.1 = f32[272,1,128]{2,1,0:T(1,128)S(1)} custom-call(f32[2,64,128]{2,1,0:T(8,128)S(1)} %collective-permute-done.table_ref, s32[16,8,128]{2,1,0:T(8,128)S(1)} %get-tuple-element.11.offsets_ref, f32[1,4096]{1,0:T(1,128)S(1)} %get-tuple-element.12.look_ref, f32[16,2,8,128]{3,2,1,0:T(8,128)S(1)} %get-tuple-element.14.own_ref, ...), custom_call_target="tpu_custom_call" | custom-call | bytes 1048576 | tf_op jit(solution)/shard_map/other_lookup/pallas_call | solution.py:217
  7.3 14.5 %all_to_all.10.terms_ref = f32[272,1,128]{2,1,0:T(1,128)S(1)} all-to-all(f32[272,1,128]{2,1,0:T(1,128)S(1)} %other_lookup.1), channel_id=1, replica_groups=mesh['pulse'=16,'tile'=4,'band'=2] {'pulse'}, dimensions={0} | all-to-all | bytes 278528 | tf_op jit(solution)/shard_map/all_to_all | solution.py:268
  21.7 0.9 %image_sums.1 = (f32[2,8,128]{2,1,0:T(8,128)S(1)}, f32[128,1,128]{2,1,0:T(1,128)}) custom-call(f32[272,1,128]{2,1,0:T(1,128)S(1)} %all_to_all.10.terms_ref), custom_call_target="tpu_custom_call" | custom-call | bytes 1048576 | tf_op jit(solution)/shard_map/image_sums/pallas_call | solution.py:217
  22.7 6.9 %all-to-all-start.1 = ((f32[128,1,128]{2,1,0:T(1,128)}), f32[128,1,128]{2,1,0:T(1,128)S(1)}, u32[]{:S(2)}, u32[]{:S(2)}) async-start(f32[128,1,128]{2,1,0:T(1,128)} %get-tuple-element.17), calls=%async_computation.1 | async-start | bytes 131072 | tf_op jit(solution)/shard_map/all_to_all | solution.py:273
  29.6 1.1 %collective-permute-start.1 = (f32[2,8,128]{2,1,0:T(8,128)S(1)}, f32[2,8,128]{2,1,0:T(8,128)S(1)}, u32[]{:S(2)}, u32[]{:S(2)}) collective-permute-start(f32[2,8,128]{2,1,0:T(8,128)S(1)} %get-tuple-element.16.own_ref), channel_id=1, source_target_pairs={{0,1},{1,0},{2,3},{3,2},{4,5},{5,4},{6,7},{7,6},{8,9},{9,8},{10,11... | collective-permute-start | bytes 24584 | tf_op jit(solution)/shard_map/ppermute | solution.py:272
  30.7 0.8 %collective-permute-done.1.other_ref = f32[2,8,128]{2,1,0:T(8,128)S(1)} collective-permute-done((f32[2,8,128]{2,1,0:T(8,128)S(1)}, f32[2,8,128]{2,1,0:T(8,128)S(1)}, u32[]{:S(2)}, u32[]{:S(2)}) %collective-permute-start.1) | collective-permute-done | bytes 8224 | tf_op jit(solution)/shard_map/ppermute | solution.py:272
  31.6 0.6 %join.1 = f32[2,8,256]{2,1,0:T(8,128)} custom-call(f32[2,8,128]{2,1,0:T(8,128)S(1)} %get-tuple-element.16.own_ref, f32[2,8,128]{2,1,0:T(8,128)S(1)} %collective-permute-done.1.other_ref), custom_call_target="tpu_custom_call" | custom-call | bytes 1048576 | tf_op jit(solution)/shard_map/join/pallas_call | solution.py:217
  32.2 6.9 %all-to-all-done.1.refs_0_ = f32[128,1,128]{2,1,0:T(1,128)S(1)} async-done(((f32[128,1,128]{2,1,0:T(1,128)}), f32[128,1,128]{2,1,0:T(1,128)S(1)}, u32[]{:S(2)}, u32[]{:S(2)}) %all-to-all-start.1) | async-done | bytes 65568 | tf_op jit(solution)/shard_map/all_to_all | solution.py:273
  39.1 0.8 %gradient.1 = f32[1,128]{1,0:T(1,128)} custom-call(f32[128,1,128]{2,1,0:T(1,128)S(1)} %all-to-all-done.1.refs_0_), custom_call_target="tpu_custom_call" | custom-call | bytes 1048576 | tf_op jit(solution)/shard_map/gradient/pallas_call | solution.py:217
Async XLA Ops:
  2.5 3.1 %collective-permute-start = (f32[2,64,128]{2,1,0:T(8,128)S(1)}, f32[2,64,128]{2,1,0:T(8,128)S(1)}, u32[]{:S(2)}, u32[]{:S(2)}) collective-permute-start(f32[2,64,128]{2,1,0:T(8,128)S(1)} %get-tuple-element.10.table_ref), channel_id=1, source_target_pairs={{0,1},{1,0},{2,3},{3,2},{4,5},{5,4},{6,7},{7,6},{8,9},{9,8},{10,11... | collective-permute-start | bytes 196616 | tf_op jit(solution)/shard_map/ppermute | solution.py:255
  22.7 16.4 %all-to-all-start.1 = ((f32[128,1,128]{2,1,0:T(1,128)}), f32[128,1,128]{2,1,0:T(1,128)S(1)}, u32[]{:S(2)}, u32[]{:S(2)}) async-start(f32[128,1,128]{2,1,0:T(1,128)} %get-tuple-element.17), calls=%async_computation.1 | async-start | bytes 131072 | tf_op jit(solution)/shard_map/all_to_all | solution.py:273
  29.6 2.0 %collective-permute-start.1 = (f32[2,8,128]{2,1,0:T(8,128)S(1)}, f32[2,8,128]{2,1,0:T(8,128)S(1)}, u32[]{:S(2)}, u32[]{:S(2)}) collective-permute-start(f32[2,8,128]{2,1,0:T(8,128)S(1)} %get-tuple-element.16.own_ref), channel_id=1, source_target_pairs={{0,1},{1,0},{2,3},{3,2},{4,5},{5,4},{6,7},{7,6},{8,9},{9,8},{10,11... | collective-permute-start | bytes 24584 | tf_op jit(solution)/shard_map/ppermute | solution.py:272

commit v3 on v2

--- a/solution.py
+++ b/solution.py
@@ -12,10 +12,9 @@
 
 LANES = 128
 ROWS_DEV = 8
-GROUP = 4
+GROUP = 16
 CHUNK = 2 * ROWS_DEV + 1
-MOST = 8191.0
-STEPS = 15
+MOST = 32767.0
 VMEM_BYTES = 8 * 1024 * 1024
 
 
@@ -93,48 +92,50 @@
 
 def pack(table_ref, words_ref):
     real, imag = table_ref[0], table_ref[1]
+    rows = real.shape[0]
     size = jnp.maximum(jnp.abs(real), jnp.abs(imag))
-    top = jnp.max(jnp.max(size, axis=0, keepdims=True), axis=1, keepdims=True)
-    top = jnp.where(top > 0.0, top, 1.0)
-    shrink = 1.0 / top
-    size = size * shrink
-    power = jnp.zeros(size.shape, jnp.int32)
-    for step in range(1, STEPS + 1):
-        power = power + jnp.where(size > 2.0**-step, 1, 0)
-    grow = (1 << (STEPS - power)).astype(jnp.float32) * MOST
-    real = jnp.floor(real * shrink * grow + 0.5).astype(jnp.int32)
-    imag = jnp.floor(imag * shrink * grow + 0.5).astype(jnp.int32)
-    words_ref[...] = (real << 18) | ((imag & 0x3FFF) << 4) | power
-    return top
-
-
-def unpack(word):
-    unit = (1 << (word & 15)).astype(jnp.float32) * (1.0 / (MOST * 2.0**STEPS))
-    return (word >> 18).astype(jnp.float32) * unit, ((word << 14) >> 18).astype(jnp.float32) * unit
-
-
-def look_up(words_ref, offsets):
+    lane = lax.broadcasted_iota(jnp.int32, size.shape, 1)
+    row = lax.broadcasted_iota(jnp.int32, size.shape, 0)
+    first_half = lane < LANES // 2
+    tops = []
+    for half in range(2):
+        inside = first_half if half == 0 else jnp.logical_not(first_half)
+        top = jnp.max(jnp.where(inside, size, 0.0), axis=1, keepdims=True)
+        tops.append(jnp.where(top > 0.0, top, 1.0))
+    shrink = jnp.where(first_half, 1.0 / tops[0], 1.0 / tops[1])
+    real = jnp.floor(real * shrink * MOST + 0.5).astype(jnp.int32)
+    imag = jnp.floor(imag * shrink * MOST + 0.5).astype(jnp.int32)
+    words_ref[...] = (real << 16) | (imag & 0xFFFF)
+    spread = jnp.where(lane == row, tops[0], 0.0) + jnp.where(lane == row + rows, tops[1], 0.0)
+    return jnp.sum(spread, axis=0, keepdims=True)
+
+
+def look_up(words_ref, tops, offsets):
+    rows = words_ref.shape[0]
     lanes = offsets & (LANES - 1)
     high = offsets >> 7
+    top = lane_lookup(jnp.broadcast_to(tops, offsets.shape), high + ((offsets & 64) * (rows // 64)))
     found = None
-    for row in range(words_ref.shape[0]):
+    for row in range(rows):
         spread = jnp.broadcast_to(words_ref[pl.ds(row, 1), :], offsets.shape)
         here = lane_lookup(spread, lanes)
         found = here if row == 0 else jnp.where(high == row, here, found)
-    return found
+    real = (found >> 16).astype(jnp.float32)
+    imag = ((found << 16) >> 16).astype(jnp.float32)
+    return real * (1.0 / MOST) * top, imag * (1.0 / MOST) * top
 
 
 def own_kernel(table_ref, offsets_ref, angle_ref, out_ref, turn_ref, words_ref):
     slabs = out_ref.shape[0]
     band = lax.axis_index("band")
-    top = pack(table_ref, words_ref)
+    tops = pack(table_ref, words_ref)
 
     def some_blocks(step, carry):
         for j in range(GROUP):
             slab = step * GROUP + j
-            real, imag = unpack(look_up(words_ref, offsets_ref[slab]))
-            out_ref[slab, 0] = top * real
-            out_ref[slab, 1] = top * imag
+            real, imag = look_up(words_ref, tops, offsets_ref[slab])
+            out_ref[slab, 0] = real
+            out_ref[slab, 1] = imag
             start = pl.multiple_of((2 * slab + band) * LANES, LANES)
             sine, cosine = sine_cosine(angle_ref[:, pl.ds(start, LANES)])
             turn_ref[slab, 0:1] = cosine
@@ -147,14 +148,14 @@
 def other_kernel(table_ref, offsets_ref, look_ref, own_ref, turn_ref, out_ref, words_ref):
     slabs = own_ref.shape[0]
     band = lax.axis_index("band")
-    top = pack(table_ref, words_ref)
+    tops = pack(table_ref, words_ref)
 
     def some_blocks(step, carry):
         for j in range(GROUP):
             slab = step * GROUP + j
-            real, imag = unpack(look_up(words_ref, offsets_ref[slab]))
-            real = own_ref[slab, 0] + top * real
-            imag = own_ref[slab, 1] + top * imag
+            real, imag = look_up(words_ref, tops, offsets_ref[slab])
+            real = own_ref[slab, 0] + real
+            imag = own_ref[slab, 1] + imag
             cosine = turn_ref[slab, 0:1]
             sine = turn_ref[slab, 1:2]
             first = slab * CHUNK

time: 40.1 us -> 39.8 us (level)
  transfers between devices with their start and end apart: 3 -> 3, of which waited for: 2 -> 2; matrix products, arithmetic and copies ran while one was open for 0% -> 0% of each run, Pallas kernels for 6% -> 5%
where the time goes in v3:
time: 39.8 us; the launch traced here: 39.5 us
  blocking collectives  14.5 us (36%)
  starting transfers between devices  9.57 us (24%)
  waiting for transfers between devices  7.74 us (19%)
  Pallas kernels  6.43 us (16%)
  between operations  1.31 us (3%)
    all_to_all x1, blocking collectives, local(): terms = lax.all_to_all(terms, 'pulse', 0, 0, tiled=True)  14.5 us
    all_to_all x1, starting transfers between devices, local(): sums = lax.all_to_all(sums, ('pulse', 'tile', 'band'), 0, 0, tiled=True)  6.92 us
    all_to_all x1, waiting for transfers between devices, local(): sums = lax.all_to_all(sums, ('pulse', 'tile', 'band'), 0, 0, tiled=True)  6.91 us
    pallas_call x6, Pallas kernels, on_device(): pl.pallas_call(kernel, out_shape=tuple((jax.ShapeDtypeStruct(shape, dtype...  6.43 us
    ppermute x1, starting transfers between devices, local(): other_table = lax.ppermute(table, 'band', swap)  1.5 us
    ppermute x1, starting transfers between devices, local(): other_half = lax.ppermute(half, 'band', swap)  1.15 us
    ppermute x1, waiting for transfers between devices, local(): other_half = lax.ppermute(half, 'band', swap)  0.83 us
  transfers between devices with their start and end apart: 3, of which 2 were waited for; matrix products, arithmetic and copies ran while one was open for 0% of the time, Pallas kernels for 5%

profile of v3, /device:TPU:1, one launch (start us, length us, event | category | flops | bytes accessed | tf_op | source)
XLA Modules:
  0.0 39.5 jit_solution(13291740233867511012)
XLA Ops:
  1.3 1.2 %table.1 = (f32[2,64,128]{2,1,0:T(8,128)S(1)}, s32[16,8,128]{2,1,0:T(8,128)S(1)}, f32[1,4096]{1,0:T(1,128)S(1)}, f32[1,4096]{1,0:T(1,128)S(1)}) custom-call(f32[1,1]{1,0:T(1,128)} %bitcast.4.delta_hbm, bf16[2,8192]{1,0:T(2,128)(2,1)} %bitcast.5, s32[1,8,4096]{2,1,0:T(8,128)} %offsets_hbm.1, f32[1,4096]{1,0:T(1,128)} %look_hbm.1), custom_call_target="tpu_custom_call" | custom-call | bytes 1048576 | tf_op jit(solution)/shard_map/table/pallas_call | solution.py:218
  2.5 1.5 %collective-permute-start = (f32[2,64,128]{2,1,0:T(8,128)S(1)}, f32[2,64,128]{2,1,0:T(8,128)S(1)}, u32[]{:S(2)}, u32[]{:S(2)}) collective-permute-start(f32[2,64,128]{2,1,0:T(8,128)S(1)} %get-tuple-element.10.table_ref), channel_id=1, source_target_pairs={{0,1},{1,0},{2,3},{3,2},{4,5},{5,4},{6,7},{7,6},{8,9},{9,8},{10,11... | collective-permute-start | bytes 196616 | tf_op jit(solution)/shard_map/ppermute | solution.py:256
  4.0 1.4 %own_lookup.1 = (f32[16,2,8,128]{3,2,1,0:T(8,128)S(1)}, f32[16,2,128]{2,1,0:T(2,128)S(1)}) custom-call(f32[2,64,128]{2,1,0:T(8,128)S(1)} %get-tuple-element.10.table_ref, s32[16,8,128]{2,1,0:T(8,128)S(1)} %get-tuple-element.11.offsets_ref, f32[1,4096]{1,0:T(1,128)S(1)} %get-tuple-element.13.angle_ref), custom_call_target="tpu_custom_call" | custom-call | flops 1073741824 | bytes 1048576 | tf_op jit(solution)/shard_map/own_lookup/pallas_call | solution.py:218
  5.5 0.0 collective-permute-done.table_ref
  5.5 1.4 %other_lookup.1 = f32[272,1,128]{2,1,0:T(1,128)S(1)} custom-call(f32[2,64,128]{2,1,0:T(8,128)S(1)} %collective-permute-done.table_ref, s32[16,8,128]{2,1,0:T(8,128)S(1)} %get-tuple-element.11.offsets_ref, f32[1,4096]{1,0:T(1,128)S(1)} %get-tuple-element.12.look_ref, f32[16,2,8,128]{3,2,1,0:T(8,128)S(1)} %get-tuple-element.14.own_ref, ...), custom_call_target="tpu_custom_call" | custom-call | bytes 1048576 | tf_op jit(solution)/shard_map/other_lookup/pallas_call | solution.py:218
  6.9 14.5 %all_to_all.10.terms_ref = f32[272,1,128]{2,1,0:T(1,128)S(1)} all-to-all(f32[272,1,128]{2,1,0:T(1,128)S(1)} %other_lookup.1), channel_id=1, replica_groups=mesh['pulse'=16,'tile'=4,'band'=2] {'pulse'}, dimensions={0} | all-to-all | bytes 278528 | tf_op jit(solution)/shard_map/all_to_all | solution.py:269
  21.3 0.9 %image_sums.1 = (f32[2,8,128]{2,1,0:T(8,128)S(1)}, f32[128,1,128]{2,1,0:T(1,128)}) custom-call(f32[272,1,128]{2,1,0:T(1,128)S(1)} %all_to_all.10.terms_ref), custom_call_target="tpu_custom_call" | custom-call | bytes 1048576 | tf_op jit(solution)/shard_map/image_sums/pallas_call | solution.py:218
  22.3 6.9 %all-to-all-start.1 = ((f32[128,1,128]{2,1,0:T(1,128)}), f32[128,1,128]{2,1,0:T(1,128)S(1)}, u32[]{:S(2)}, u32[]{:S(2)}) async-start(f32[128,1,128]{2,1,0:T(1,128)} %get-tuple-element.17), calls=%async_computation.1 | async-start | bytes 131072 | tf_op jit(solution)/shard_map/all_to_all | solution.py:274
  29.2 1.1 %collective-permute-start.1 = (f32[2,8,128]{2,1,0:T(8,128)S(1)}, f32[2,8,128]{2,1,0:T(8,128)S(1)}, u32[]{:S(2)}, u32[]{:S(2)}) collective-permute-start(f32[2,8,128]{2,1,0:T(8,128)S(1)} %get-tuple-element.16.own_ref), channel_id=1, source_target_pairs={{0,1},{1,0},{2,3},{3,2},{4,5},{5,4},{6,7},{7,6},{8,9},{9,8},{10,11... | collective-permute-start | bytes 24584 | tf_op jit(solution)/shard_map/ppermute | solution.py:273
  30.4 0.8 %collective-permute-done.1.other_ref = f32[2,8,128]{2,1,0:T(8,128)S(1)} collective-permute-done((f32[2,8,128]{2,1,0:T(8,128)S(1)}, f32[2,8,128]{2,1,0:T(8,128)S(1)}, u32[]{:S(2)}, u32[]{:S(2)}) %collective-permute-start.1) | collective-permute-done | bytes 8224 | tf_op jit(solution)/shard_map/ppermute | solution.py:273
  31.2 0.6 %join.1 = f32[2,8,256]{2,1,0:T(8,128)} custom-call(f32[2,8,128]{2,1,0:T(8,128)S(1)} %get-tuple-element.16.own_ref, f32[2,8,128]{2,1,0:T(8,128)S(1)} %collective-permute-done.1.other_ref), custom_call_target="tpu_custom_call" | custom-call | bytes 1048576 | tf_op jit(solution)/shard_map/join/pallas_call | solution.py:218
  31.8 6.9 %all-to-all-done.1.refs_0_ = f32[128,1,128]{2,1,0:T(1,128)S(1)} async-done(((f32[128,1,128]{2,1,0:T(1,128)}), f32[128,1,128]{2,1,0:T(1,128)S(1)}, u32[]{:S(2)}, u32[]{:S(2)}) %all-to-all-start.1) | async-done | bytes 65568 | tf_op jit(solution)/shard_map/all_to_all | solution.py:274
  38.7 0.8 %gradient.1 = f32[1,128]{1,0:T(1,128)} custom-call(f32[128,1,128]{2,1,0:T(1,128)S(1)} %all-to-all-done.1.refs_0_), custom_call_target="tpu_custom_call" | custom-call | bytes 1048576 | tf_op jit(solution)/shard_map/gradient/pallas_call | solution.py:218
Async XLA Ops:
  2.5 2.9 %collective-permute-start = (f32[2,64,128]{2,1,0:T(8,128)S(1)}, f32[2,64,128]{2,1,0:T(8,128)S(1)}, u32[]{:S(2)}, u32[]{:S(2)}) collective-permute-start(f32[2,64,128]{2,1,0:T(8,128)S(1)} %get-tuple-element.10.table_ref), channel_id=1, source_target_pairs={{0,1},{1,0},{2,3},{3,2},{4,5},{5,4},{6,7},{7,6},{8,9},{9,8},{10,11... | collective-permute-start | bytes 196616 | tf_op jit(solution)/shard_map/ppermute | solution.py:256
  22.3 16.4 %all-to-all-start.1 = ((f32[128,1,128]{2,1,0:T(1,128)}), f32[128,1,128]{2,1,0:T(1,128)S(1)}, u32[]{:S(2)}, u32[]{:S(2)}) async-start(f32[128,1,128]{2,1,0:T(1,128)} %get-tuple-element.17), calls=%async_computation.1 | async-start | bytes 131072 | tf_op jit(solution)/shard_map/all_to_all | solution.py:274
  29.2 2.0 %collective-permute-start.1 = (f32[2,8,128]{2,1,0:T(8,128)S(1)}, f32[2,8,128]{2,1,0:T(8,128)S(1)}, u32[]{:S(2)}, u32[]{:S(2)}) collective-permute-start(f32[2,8,128]{2,1,0:T(8,128)S(1)} %get-tuple-element.16.own_ref), channel_id=1, source_target_pairs={{0,1},{1,0},{2,3},{3,2},{4,5},{5,4},{6,7},{7,6},{8,9},{9,8},{10,11... | collective-permute-start | bytes 24584 | tf_op jit(solution)/shard_map/ppermute | solution.py:273

commit v4 on v3

--- a/solution.py
+++ b/solution.py
@@ -12,9 +12,9 @@
 
 LANES = 128
 ROWS_DEV = 8
-GROUP = 16
 CHUNK = 2 * ROWS_DEV + 1
 MOST = 32767.0
+CHAIN = 16
 VMEM_BYTES = 8 * 1024 * 1024
 
 
@@ -56,20 +56,16 @@
     return jnp.take_along_axis(row, lanes, axis=1, mode="promise_in_bounds")
 
 
-def table_kernel(
-    delta_hbm, echo_hbm, offsets_hbm, look_hbm, table_ref, offsets_ref, look_ref, angle_ref, echo_ref, delta_ref, arrived
-):
+def table_kernel(echo_hbm, offsets_hbm, look_hbm, table_ref, offsets_ref, look_ref, echo_ref, arrived):
     band = lax.axis_index("band")
-    slabs = offsets_ref.shape[0]
-    copies = [pltpu.make_async_copy(echo_hbm, echo_ref, arrived.at[0])]
-    copies.append(pltpu.make_async_copy(look_hbm, look_ref, arrived.at[1]))
-    copies.append(pltpu.make_async_copy(delta_hbm, delta_ref, arrived.at[2]))
-    for slab in range(slabs):
-        start = pl.multiple_of((2 * slab + band) * LANES, LANES)
+    copies = [
+        pltpu.make_async_copy(echo_hbm, echo_ref, arrived.at[0]),
+        pltpu.make_async_copy(look_hbm, look_ref, arrived.at[1]),
+    ]
+    for slab in range(offsets_ref.shape[0]):
+        block = pl.ds(pl.multiple_of((2 * slab + band) * LANES, LANES), LANES)
         copies.append(
-            pltpu.make_async_copy(
-                offsets_hbm.at[0, :, pl.ds(start, LANES)], offsets_ref.at[slab], arrived.at[3 + slab]
-            )
+            pltpu.make_async_copy(offsets_hbm.at[0, :, block], offsets_ref.at[slab], arrived.at[2 + slab])
         )
     for copy in copies:
         copy.start()
@@ -83,15 +79,21 @@
         filt.append(filtered_rows(rows))
     table_ref[0] = cosine * filt[0] - sine * filt[1]
     table_ref[1] = sine * filt[0] + cosine * filt[1]
-    copies[1].wait()
-    copies[2].wait()
-    angle_ref[...] = delta_ref[...] * look_ref[...]
-    for copy in copies[3:]:
+    for copy in copies[1:]:
         copy.wait()
 
 
-def pack(table_ref, words_ref):
-    real, imag = table_ref[0], table_ref[1]
+def turn_kernel(delta_ref, look_ref, own_look_ref, turn_ref):
+    band = lax.axis_index("band")
+    for slab in range(own_look_ref.shape[0]):
+        block = pl.ds(pl.multiple_of((2 * slab + band) * LANES, LANES), LANES)
+        own_look_ref[slab : slab + 1] = look_ref[:, block]
+    sine, cosine = sine_cosine(delta_ref[0] * own_look_ref[...])
+    turn_ref[0] = cosine
+    turn_ref[1] = sine
+
+
+def pack(real, imag, words_ref):
     rows = real.shape[0]
     size = jnp.maximum(jnp.abs(real), jnp.abs(imag))
     lane = lax.broadcasted_iota(jnp.int32, size.shape, 1)
@@ -115,57 +117,32 @@
     lanes = offsets & (LANES - 1)
     high = offsets >> 7
     top = lane_lookup(jnp.broadcast_to(tops, offsets.shape), high + ((offsets & 64) * (rows // 64)))
-    found = None
-    for row in range(rows):
-        spread = jnp.broadcast_to(words_ref[pl.ds(row, 1), :], offsets.shape)
-        here = lane_lookup(spread, lanes)
-        found = here if row == 0 else jnp.where(high == row, here, found)
+    low = high & (CHAIN - 1)
+    chains = [None] * (rows // CHAIN)
+    for step in range(CHAIN):
+        match = low == step
+        for chain in range(len(chains)):
+            row = chain * CHAIN + step
+            here = lane_lookup(jnp.broadcast_to(words_ref[pl.ds(row, 1), :], offsets.shape), lanes)
+            chains[chain] = here if step == 0 else jnp.where(match, here, chains[chain])
+    found = chains[0]
+    for chain in range(1, len(chains)):
+        found = jnp.where(high >= chain * CHAIN, chains[chain], found)
     real = (found >> 16).astype(jnp.float32)
     imag = ((found << 16) >> 16).astype(jnp.float32)
     return real * (1.0 / MOST) * top, imag * (1.0 / MOST) * top
 
 
-def own_kernel(table_ref, offsets_ref, angle_ref, out_ref, turn_ref, words_ref):
-    slabs = out_ref.shape[0]
-    band = lax.axis_index("band")
-    tops = pack(table_ref, words_ref)
-
-    def some_blocks(step, carry):
-        for j in range(GROUP):
-            slab = step * GROUP + j
-            real, imag = look_up(words_ref, tops, offsets_ref[slab])
-            out_ref[slab, 0] = real
-            out_ref[slab, 1] = imag
-            start = pl.multiple_of((2 * slab + band) * LANES, LANES)
-            sine, cosine = sine_cosine(angle_ref[:, pl.ds(start, LANES)])
-            turn_ref[slab, 0:1] = cosine
-            turn_ref[slab, 1:2] = sine
-        return carry
-
-    lax.fori_loop(0, slabs // GROUP, some_blocks, 0)
-
-
-def other_kernel(table_ref, offsets_ref, look_ref, own_ref, turn_ref, out_ref, words_ref):
-    slabs = own_ref.shape[0]
-    band = lax.axis_index("band")
-    tops = pack(table_ref, words_ref)
-
-    def some_blocks(step, carry):
-        for j in range(GROUP):
-            slab = step * GROUP + j
-            real, imag = look_up(words_ref, tops, offsets_ref[slab])
-            real = own_ref[slab, 0] + real
-            imag = own_ref[slab, 1] + imag
-            cosine = turn_ref[slab, 0:1]
-            sine = turn_ref[slab, 1:2]
-            first = slab * CHUNK
-            out_ref[pl.ds(first, ROWS_DEV), 0, :] = cosine * real - sine * imag
-            out_ref[pl.ds(first + ROWS_DEV, ROWS_DEV), 0, :] = sine * real + cosine * imag
-            start = pl.multiple_of((2 * slab + band) * LANES, LANES)
-            out_ref[first + 2 * ROWS_DEV] = look_ref[:, pl.ds(start, LANES)]
-        return carry
-
-    lax.fori_loop(0, slabs // GROUP, some_blocks, 0)
+def terms_kernel(own_ref, other_ref, offsets_ref, look_ref, turn_ref, out_ref, words_ref):
+    tops = pack(own_ref[0] + other_ref[0], own_ref[1] + other_ref[1], words_ref)
+    for slab in range(offsets_ref.shape[0]):
+        real, imag = look_up(words_ref, tops, offsets_ref[slab])
+        cosine = turn_ref[0, slab : slab + 1]
+        sine = turn_ref[1, slab : slab + 1]
+        first = slab * CHUNK
+        out_ref[first : first + ROWS_DEV, 0, :] = cosine * real - sine * imag
+        out_ref[first + ROWS_DEV : first + 2 * ROWS_DEV, 0, :] = sine * real + cosine * imag
+        out_ref[first + 2 * ROWS_DEV] = look_ref[slab : slab + 1]
 
 
 def image_kernel(terms_ref, image_ref, sums_ref):
@@ -191,8 +168,8 @@
     lane = lax.broadcasted_iota(jnp.int32, (pulses, LANES), 1)
     sums = jnp.where(lane == 0, power_cross_sums, 0.0) + jnp.where(lane == 1, cross_sums, 0.0)
     sums = sums + jnp.where(lane == 2, power_sum, 0.0) + jnp.where(lane == 3, quart_sum, 0.0)
-    for p in range(pulses):
-        sums_ref[p * copies : (p + 1) * copies, 0, :] = jnp.broadcast_to(sums[p : p + 1], (copies, LANES))
+    for copy in range(copies):
+        sums_ref[copy * pulses : (copy + 1) * pulses, 0, :] = sums
 
 
 def join_kernel(own_ref, other_ref, image_ref):
@@ -238,40 +215,36 @@
     swap = [(0, 1), (1, 0)]
     f32, i32 = jnp.float32, jnp.int32
     table_shape = (2, bins // LANES, LANES)
-    words = pltpu.VMEM(table_shape[1:], i32)
     half_shape = (2, rows_dev, LANES)
-
-    inputs = (delta.reshape(1, 1), echo.reshape(2, bins), offsets, look)
-    table, own_offsets, look, angle = on_device(
+    columns_shape = (slabs, LANES)
+
+    inputs = (echo.reshape(2, bins), offsets, look)
+    table, own_offsets, look = on_device(
         table_kernel,
-        [(table_shape, f32), ((slabs, rows_dev, LANES), i32), ((1, columns), f32), ((1, columns), f32)],
-        inputs[0], *(pltpu.with_memory_space_constraint(array, pltpu.HBM) for array in inputs[1:]),
-        name="table", spaces=[pl.BlockSpec(memory_space=pl.ANY)] + [HBM] * 3,
-        scratch=[
-            pltpu.VMEM((2, bins), echo.dtype),
-            pltpu.VMEM((1, 1), f32),
-            pltpu.SemaphoreType.DMA((3 + slabs,)),
-        ],
+        [(table_shape, f32), ((slabs, rows_dev, LANES), i32), ((1, columns), f32)],
+        *(pltpu.with_memory_space_constraint(array, pltpu.HBM) for array in inputs),
+        name="table", spaces=[HBM] * 3,
+        scratch=[pltpu.VMEM((2, bins), echo.dtype), pltpu.SemaphoreType.DMA((2 + slabs,))],
     )
     other_table = lax.ppermute(table, "band", swap)
-    own, turn = on_device(
-        own_kernel,
-        [((slabs,) + half_shape, f32), ((slabs, 2, LANES), f32)],
-        table, own_offsets, angle,
-        name="own_lookup", scratch=[words], flops=1 << 30,
+    own_look, turn = on_device(
+        turn_kernel,
+        [(columns_shape, f32), ((2,) + columns_shape, f32)],
+        delta, look,
+        name="turn", spaces=[SMEM, VMEM], flops=1 << 30,
     )
     (terms,) = on_device(
-        other_kernel,
+        terms_kernel,
         [((slabs * CHUNK, 1, LANES), f32)],
-        other_table, own_offsets, look, own, turn,
-        name="other_lookup", scratch=[words],
+        table, other_table, own_offsets, own_look, turn,
+        name="terms", scratch=[pltpu.VMEM(table_shape[1:], i32)],
     )
     terms = lax.all_to_all(terms, "pulse", 0, 0, tiled=True)
     half, sums = on_device(
         image_kernel, [(half_shape, f32), ((pulses * tiles * bands, 1, LANES), f32)], terms, name="image_sums"
     )
     other_half = lax.ppermute(half, "band", swap)
-    sums = lax.all_to_all(sums, ("pulse", "tile", "band"), 0, 0, tiled=True)
+    sums = lax.all_to_all(sums, ("band", "tile", "pulse"), 0, 0, tiled=True)
     (image,) = on_device(join_kernel, [((2, rows_dev, 2 * LANES), f32)], half, other_half, name="join")
     (gradient,) = on_device(
         lambda *refs: gradient_kernel(*refs, pulses=pulses, npix=npix), [((1, LANES), f32)], sums, name="gradient"

time: 39.8 us -> 38.7 us (0.972)
  Pallas kernels: 6.43 us -> 4.98 us
  starting transfers between devices: 9.57 us -> 10 us
    pallas_call x6, Pallas kernels: 6.43 us -> 4.98 us  [on_device(): pl.pallas_call(kernel, out_shape=tuple((jax.ShapeDtypeStruct(shape, dtype...]
    all_to_all x1, starting transfers between devices: 6.92 us -> 7.35 us  [local(): sums = lax.all_to_all(sums, ('band', 'tile', 'pulse'), 0, 0, tiled=True)]
  transfers between devices with their start and end apart: 3 -> 3, of which waited for: 2 -> 3; matrix products, arithmetic and copies ran while one was open for 0% -> 0% of each run, Pallas kernels for 5% -> 2%
where the time goes in v4:
time: 38.7 us; the launch traced here: 38.4 us
  blocking collectives  14.4 us (37%)
  starting transfers between devices  10 us (26%)
  waiting for transfers between devices  7.77 us (20%)
  Pallas kernels  4.98 us (13%)
  between operations  1.31 us (3%)
    all_to_all x1, blocking collectives, local(): terms = lax.all_to_all(terms, 'pulse', 0, 0, tiled=True)  14.4 us
    all_to_all x1, starting transfers between devices, local(): sums = lax.all_to_all(sums, ('band', 'tile', 'pulse'), 0, 0, tiled=True)  7.35 us
    all_to_all x1, waiting for transfers between devices, local(): sums = lax.all_to_all(sums, ('band', 'tile', 'pulse'), 0, 0, tiled=True)  6.74 us
    pallas_call x6, Pallas kernels, on_device(): pl.pallas_call(kernel, out_shape=tuple((jax.ShapeDtypeStruct(shape, dtype...  4.98 us
    ppermute x1, starting transfers between devices, local(): other_table = lax.ppermute(table, 'band', swap)  1.5 us
    ppermute x1, starting transfers between devices, local(): other_half = lax.ppermute(half, 'band', swap)  1.15 us
    ppermute x1, waiting for transfers between devices, local(): other_half = lax.ppermute(half, 'band', swap)  0.83 us
  transfers between devices with their start and end apart: 3, of which 3 were waited for; matrix products, arithmetic and copies ran while one was open for 0% of the time, Pallas kernels for 2%

profile of v4, /device:TPU:1, one launch (start us, length us, event | category | flops | bytes accessed | tf_op | source)
XLA Modules:
  0.0 38.4 jit_solution(14932933507327854653)
XLA Ops:
  0.6 1.1 %table.1 = (f32[2,64,128]{2,1,0:T(8,128)S(1)}, s32[16,8,128]{2,1,0:T(8,128)S(1)}, f32[1,4096]{1,0:T(1,128)S(1)}) custom-call(bf16[2,8192]{1,0:T(2,128)(2,1)} %bitcast.3, s32[1,8,4096]{2,1,0:T(8,128)} %offsets_hbm.1, f32[1,4096]{1,0:T(1,128)} %look_hbm.1), custom_call_target="tpu_custom_call" | custom-call | bytes 1048576 | tf_op jit(solution)/shard_map/table/pallas_call | solution.py:195
  1.8 1.5 %collective-permute-start = (f32[2,64,128]{2,1,0:T(8,128)S(1)}, f32[2,64,128]{2,1,0:T(8,128)S(1)}, u32[]{:S(2)}, u32[]{:S(2)}) collective-permute-start(f32[2,64,128]{2,1,0:T(8,128)S(1)} %get-tuple-element.9.own_ref), channel_id=1, source_target_pairs={{0,1},{1,0},{2,3},{3,2},{4,5},{5,4},{6,7},{7,6},{8,9},{9,8},{10,11... | collective-permute-start | bytes 196616 | tf_op jit(solution)/shard_map/ppermute | solution.py:229
  4.0 0.2 collective-permute-done.other_ref
  4.2 1.4 %terms.1 = f32[272,1,128]{2,1,0:T(1,128)S(1)} custom-call(f32[2,64,128]{2,1,0:T(8,128)S(1)} %get-tuple-element.9.own_ref, f32[2,64,128]{2,1,0:T(8,128)S(1)} %collective-permute-done.other_ref, s32[16,8,128]{2,1,0:T(8,128)S(1)} %get-tuple-element.10.offsets_ref, f32[16,128]{1,0:T(8,128)S(1)} %get-tuple-element.12.look_ref, ...), custom_call_target="tpu_custom_call" | custom-call | bytes 1048576 | tf_op jit(solution)/shard_map/terms/pallas_call | solution.py:195
  5.6 14.4 %all_to_all.10.terms_ref = f32[272,1,128]{2,1,0:T(1,128)S(1)} all-to-all(f32[272,1,128]{2,1,0:T(1,128)S(1)} %terms.1), channel_id=1, replica_groups=mesh['pulse'=16,'tile'=4,'band'=2] {'pulse'}, dimensions={0} | all-to-all | bytes 278528 | tf_op jit(solution)/shard_map/all_to_all | solution.py:242
  20.0 1.0 %image_sums.1 = (f32[2,8,128]{2,1,0:T(8,128)S(1)}, f32[128,1,128]{2,1,0:T(1,128)}) custom-call(f32[272,1,128]{2,1,0:T(1,128)S(1)} %all_to_all.10.terms_ref), custom_call_target="tpu_custom_call" | custom-call | bytes 1048576 | tf_op jit(solution)/shard_map/image_sums/pallas_call | solution.py:195
  20.9 7.3 %all-to-all-start.1 = ((f32[128,1,128]{2,1,0:T(1,128)}), f32[128,1,128]{2,1,0:T(1,128)S(1)}, u32[]{:S(2)}, u32[]{:S(2)}) async-start(f32[128,1,128]{2,1,0:T(1,128)} %get-tuple-element.15), calls=%async_computation.1 | async-start | bytes 131072 | tf_op jit(solution)/shard_map/all_to_all | solution.py:247
  28.3 1.1 %collective-permute-start.1 = (f32[2,8,128]{2,1,0:T(8,128)S(1)}, f32[2,8,128]{2,1,0:T(8,128)S(1)}, u32[]{:S(2)}, u32[]{:S(2)}) collective-permute-start(f32[2,8,128]{2,1,0:T(8,128)S(1)} %get-tuple-element.14.own_ref), channel_id=1, source_target_pairs={{0,1},{1,0},{2,3},{3,2},{4,5},{5,4},{6,7},{7,6},{8,9},{9,8},{10,11... | collective-permute-start | bytes 24584 | tf_op jit(solution)/shard_map/ppermute | solution.py:246
  29.4 0.8 %collective-permute-done.1.other_ref = f32[2,8,128]{2,1,0:T(8,128)S(1)} collective-permute-done((f32[2,8,128]{2,1,0:T(8,128)S(1)}, f32[2,8,128]{2,1,0:T(8,128)S(1)}, u32[]{:S(2)}, u32[]{:S(2)}) %collective-permute-start.1) | collective-permute-done | bytes 8224 | tf_op jit(solution)/shard_map/ppermute | solution.py:246
  30.3 0.6 %join.1 = f32[2,8,256]{2,1,0:T(8,128)} custom-call(f32[2,8,128]{2,1,0:T(8,128)S(1)} %get-tuple-element.14.own_ref, f32[2,8,128]{2,1,0:T(8,128)S(1)} %collective-permute-done.1.other_ref), custom_call_target="tpu_custom_call" | custom-call | bytes 1048576 | tf_op jit(solution)/shard_map/join/pallas_call | solution.py:195
  30.9 6.7 %all-to-all-done.1.refs_0_ = f32[128,1,128]{2,1,0:T(1,128)S(1)} async-done(((f32[128,1,128]{2,1,0:T(1,128)}), f32[128,1,128]{2,1,0:T(1,128)S(1)}, u32[]{:S(2)}, u32[]{:S(2)}) %all-to-all-start.1) | async-done | bytes 65568 | tf_op jit(solution)/shard_map/all_to_all | solution.py:247
  37.6 0.8 %gradient.1 = f32[1,128]{1,0:T(1,128)} custom-call(f32[128,1,128]{2,1,0:T(1,128)S(1)} %all-to-all-done.1.refs_0_), custom_call_target="tpu_custom_call" | custom-call | bytes 1048576 | tf_op jit(solution)/shard_map/gradient/pallas_call | solution.py:195
  (1 shorter events, 0.0 us)
Async XLA Ops:
  1.8 2.4 %collective-permute-start = (f32[2,64,128]{2,1,0:T(8,128)S(1)}, f32[2,64,128]{2,1,0:T(8,128)S(1)}, u32[]{:S(2)}, u32[]{:S(2)}) collective-permute-start(f32[2,64,128]{2,1,0:T(8,128)S(1)} %get-tuple-element.9.own_ref), channel_id=1, source_target_pairs={{0,1},{1,0},{2,3},{3,2},{4,5},{5,4},{6,7},{7,6},{8,9},{9,8},{10,11... | collective-permute-start | bytes 196616 | tf_op jit(solution)/shard_map/ppermute | solution.py:229
  20.9 16.7 %all-to-all-start.1 = ((f32[128,1,128]{2,1,0:T(1,128)}), f32[128,1,128]{2,1,0:T(1,128)S(1)}, u32[]{:S(2)}, u32[]{:S(2)}) async-start(f32[128,1,128]{2,1,0:T(1,128)} %get-tuple-element.15), calls=%async_computation.1 | async-start | bytes 131072 | tf_op jit(solution)/shard_map/all_to_all | solution.py:247
  28.3 2.0 %collective-permute-start.1 = (f32[2,8,128]{2,1,0:T(8,128)S(1)}, f32[2,8,128]{2,1,0:T(8,128)S(1)}, u32[]{:S(2)}, u32[]{:S(2)}) collective-permute-start(f32[2,8,128]{2,1,0:T(8,128)S(1)} %get-tuple-element.14.own_ref), channel_id=1, source_target_pairs={{0,1},{1,0},{2,3},{3,2},{4,5},{5,4},{6,7},{7,6},{8,9},{9,8},{10,11... | collective-permute-start | bytes 24584 | tf_op jit(solution)/shard_map/ppermute | solution.py:246

commit v5 on v4

--- a/solution.py
+++ b/solution.py
@@ -145,11 +145,17 @@
         out_ref[first + 2 * ROWS_DEV] = look_ref[slab : slab + 1]
 
 
+def chunk_parts(terms_ref, part):
+    first = part * ROWS_DEV
+    starts = range(first, terms_ref.shape[0], CHUNK)
+    return [terms_ref[start : start + ROWS_DEV, 0, :] for start in starts]
+
+
 def image_kernel(terms_ref, image_ref, sums_ref):
     pulses = terms_ref.shape[0] // CHUNK
     copies = sums_ref.shape[0] // pulses
-    reals = [terms_ref[p * CHUNK : p * CHUNK + ROWS_DEV, 0, :] for p in range(pulses)]
-    imags = [terms_ref[p * CHUNK + ROWS_DEV : p * CHUNK + 2 * ROWS_DEV, 0, :] for p in range(pulses)]
+    reals = chunk_parts(terms_ref, 0)
+    imags = chunk_parts(terms_ref, 1)
     looks = [terms_ref[p * CHUNK + 2 * ROWS_DEV] for p in range(pulses)]
     real = sum(reals[1:], reals[0])
     imag = sum(imags[1:], imags[0])
@@ -172,13 +178,18 @@
         sums_ref[copy * pulses : (copy + 1) * pulses, 0, :] = sums
 
 
-def join_kernel(own_ref, other_ref, image_ref):
+def join(own_ref, other_terms_ref, image_ref):
     band = lax.axis_index("band")
-    image_ref[:, :, 0:LANES] = jnp.where(band == 0, own_ref[...], other_ref[...])
-    image_ref[:, :, LANES:] = jnp.where(band == 0, other_ref[...], own_ref[...])
-
-
-def gradient_kernel(sums_ref, gradient_ref, *, pulses, npix):
+    for part in range(2):
+        own = own_ref[part]
+        parts = chunk_parts(other_terms_ref, part)
+        other = sum(parts[1:], parts[0])
+        image_ref[part, :, 0:LANES] = jnp.where(band == 0, own, other)
+        image_ref[part, :, LANES:] = jnp.where(band == 0, other, own)
+
+
+def gradient_kernel(own_ref, other_ref, sums_ref, gradient_ref, image_ref, *, pulses, npix):
+    join(own_ref, other_ref, image_ref)
     totals = jnp.sum(sums_ref[:, 0, :], axis=0, keepdims=True)
     mean_power = totals[:, 2:3] / npix + power_floor
     quart = totals[:, 3:4] / npix
@@ -240,14 +251,15 @@
         name="terms", scratch=[pltpu.VMEM(table_shape[1:], i32)],
     )
     terms = lax.all_to_all(terms, "pulse", 0, 0, tiled=True)
+    other_terms = lax.ppermute(terms, "band", swap)
     half, sums = on_device(
         image_kernel, [(half_shape, f32), ((pulses * tiles * bands, 1, LANES), f32)], terms, name="image_sums"
     )
-    other_half = lax.ppermute(half, "band", swap)
     sums = lax.all_to_all(sums, ("band", "tile", "pulse"), 0, 0, tiled=True)
-    (image,) = on_device(join_kernel, [((2, rows_dev, 2 * LANES), f32)], half, other_half, name="join")
-    (gradient,) = on_device(
-        lambda *refs: gradient_kernel(*refs, pulses=pulses, npix=npix), [((1, LANES), f32)], sums, name="gradient"
+    gradient, image = on_device(
+        lambda *refs: gradient_kernel(*refs, pulses=pulses, npix=npix),
+        [((1, LANES), f32), ((2, rows_dev, 2 * LANES), f32)],
+        half, other_terms, sums, name="gradient",
     )
     return image, gradient[0, 0:1]
 

time: 38.7 us -> 38 us (0.982)
  blocking collectives: 14.4 us -> 29.2 us
  waiting for transfers between devices: 7.77 us -> 0.2 us
  starting transfers between devices: 10 us -> 3.28 us
  Pallas kernels: 4.98 us -> 3.76 us
    all_to_all x0 -> x1, blocking collectives: none -> 14.8 us  [local(): sums = lax.all_to_all(sums, ('band', 'tile', 'pulse'), 0, 0, tiled=True)]
    all_to_all x1 -> x0, starting transfers between devices: 7.35 us -> none  [local(): sums = lax.all_to_all(sums, ('band', 'tile', 'pulse'), 0, 0, tiled=True)]
    all_to_all x1 -> x0, waiting for transfers between devices: 6.74 us -> none  [local(): sums = lax.all_to_all(sums, ('band', 'tile', 'pulse'), 0, 0, tiled=True)]
    pallas_call x6 -> x5, Pallas kernels: 4.98 us -> 3.76 us  [on_device(): pl.pallas_call(kernel, out_shape=tuple((jax.ShapeDtypeStruct(shape, dtype...]
    ppermute x1, waiting for transfers between devices: 0.83 us -> 0.01 us  [local(): other_terms = lax.ppermute(terms, 'band', swap)]
    ppermute x1, starting transfers between devices: 1.15 us -> 1.78 us  [local(): other_terms = lax.ppermute(terms, 'band', swap)]
  transfers between devices with their start and end apart: 3 -> 2, of which waited for: 3 -> 1; matrix products, arithmetic and copies ran while one was open for 0% -> 0% of each run, Pallas kernels for 2% -> 1%
where the time goes in v5:
time: 38 us; the launch traced here: 37.7 us
  blocking collectives  29.2 us (77%)
  Pallas kernels  3.76 us (10%)
  starting transfers between devices  3.28 us (9%)
  between operations  1.3 us (3%)
    all_to_all x1, blocking collectives, local(): sums = lax.all_to_all(sums, ('band', 'tile', 'pulse'), 0, 0, tiled=True)  14.8 us
    all_to_all x1, blocking collectives, local(): terms = lax.all_to_all(terms, 'pulse', 0, 0, tiled=True)  14.4 us
    pallas_call x5, Pallas kernels, on_device(): pl.pallas_call(kernel, out_shape=tuple((jax.ShapeDtypeStruct(shape, dtype...  3.76 us
    ppermute x1, starting transfers between devices, local(): other_terms = lax.ppermute(terms, 'band', swap)  1.78 us
    ppermute x1, starting transfers between devices, local(): other_table = lax.ppermute(table, 'band', swap)  1.5 us
  transfers between devices with their start and end apart: 2, of which 1 were waited for; matrix products, arithmetic and copies ran while one was open for 0% of the time, Pallas kernels for 1%

profile of v5, /device:TPU:1, one launch (start us, length us, event | category | flops | bytes accessed | tf_op | source)
XLA Modules:
  0.0 37.7 jit_solution(16290569322832265785)
XLA Ops:
  0.6 1.1 %table.1 = (f32[2,64,128]{2,1,0:T(8,128)S(1)}, s32[16,8,128]{2,1,0:T(8,128)S(1)}, f32[1,4096]{1,0:T(1,128)S(1)}) custom-call(bf16[2,8192]{1,0:T(2,128)(2,1)} %bitcast.3, s32[1,8,4096]{2,1,0:T(8,128)} %offsets_hbm.1, f32[1,4096]{1,0:T(1,128)} %look_hbm.1), custom_call_target="tpu_custom_call" | custom-call | bytes 1048576 | tf_op jit(solution)/shard_map/table/pallas_call | solution.py:206
  1.8 1.5 %collective-permute-start = (f32[2,64,128]{2,1,0:T(8,128)S(1)}, f32[2,64,128]{2,1,0:T(8,128)S(1)}, u32[]{:S(2)}, u32[]{:S(2)}) collective-permute-start(f32[2,64,128]{2,1,0:T(8,128)S(1)} %get-tuple-element.11.own_ref), channel_id=1, source_target_pairs={{0,1},{1,0},{2,3},{3,2},{4,5},{5,4},{6,7},{7,6},{8,9},{9,8},{10,11... | collective-permute-start | bytes 196616 | tf_op jit(solution)/shard_map/ppermute | solution.py:240
  4.0 0.2 collective-permute-done.other_ref
  4.2 1.4 %terms.1 = f32[272,1,128]{2,1,0:T(1,128)S(1)} custom-call(f32[2,64,128]{2,1,0:T(8,128)S(1)} %get-tuple-element.11.own_ref, f32[2,64,128]{2,1,0:T(8,128)S(1)} %collective-permute-done.other_ref, s32[16,8,128]{2,1,0:T(8,128)S(1)} %get-tuple-element.12.offsets_ref, f32[16,128]{1,0:T(8,128)S(1)} %get-tuple-element.14.look_ref, ...), custom_call_target="tpu_custom_call" | custom-call | bytes 1048576 | tf_op jit(solution)/shard_map/terms/pallas_call | solution.py:206
  5.6 14.4 %all_to_all.10.terms_ref = f32[272,1,128]{2,1,0:T(1,128)S(1)} all-to-all(f32[272,1,128]{2,1,0:T(1,128)S(1)} %terms.1), channel_id=1, replica_groups=mesh['pulse'=16,'tile'=4,'band'=2] {'pulse'}, dimensions={0} | all-to-all | bytes 278528 | tf_op jit(solution)/shard_map/all_to_all | solution.py:253
  20.0 1.8 %collective-permute-start.1 = (f32[272,1,128]{2,1,0:T(1,128)S(1)}, f32[272,1,128]{2,1,0:T(1,128)S(1)}, u32[]{:S(2)}, u32[]{:S(2)}) collective-permute-start(f32[272,1,128]{2,1,0:T(1,128)S(1)} %all_to_all.10.terms_ref), channel_id=1, source_target_pairs={{0,1},{1,0},{2,3},{3,2},{4,5},{5,4},{6,7},{7,6},{8,9},{9,8},{10,11... | collective-permute-start | bytes 417800 | tf_op jit(solution)/shard_map/ppermute | solution.py:254
  21.7 0.3 image_sums.1
  22.1 14.8 %all_to_all.11.refs_2_ = f32[128,1,128]{2,1,0:T(1,128)S(1)} all-to-all(f32[128,1,128]{2,1,0:T(1,128)S(1)} %get-tuple-element.17), channel_id=1, replica_groups=mesh['pulse'=16,'tile'=4,'band'=2] {'band','tile','pulse'}, dimensions={0} | all-to-all | bytes 131072 | tf_op jit(solution)/shard_map/all_to_all | solution.py:258
  36.9 0.0 collective-permute-done.1.refs_1_
  36.9 0.8 %gradient.1 = (f32[1,128]{1,0:T(1,128)}, f32[2,8,256]{2,1,0:T(8,128)}) custom-call(f32[2,8,128]{2,1,0:T(8,128)S(1)} %get-tuple-element.16.refs_0_, f32[272,1,128]{2,1,0:T(1,128)S(1)} %collective-permute-done.1.refs_1_, f32[128,1,128]{2,1,0:T(1,128)S(1)} %all_to_all.11.refs_2_), custom_call_target="tpu_custom_call" | custom-call | bytes 1048576 | tf_op jit(solution)/shard_map/gradient/pallas_call | solution.py:206
  (1 shorter events, 0.0 us)
Async XLA Ops:
  1.8 2.4 %collective-permute-start = (f32[2,64,128]{2,1,0:T(8,128)S(1)}, f32[2,64,128]{2,1,0:T(8,128)S(1)}, u32[]{:S(2)}, u32[]{:S(2)}) collective-permute-start(f32[2,64,128]{2,1,0:T(8,128)S(1)} %get-tuple-element.11.own_ref), channel_id=1, source_target_pairs={{0,1},{1,0},{2,3},{3,2},{4,5},{5,4},{6,7},{7,6},{8,9},{9,8},{10,11... | collective-permute-start | bytes 196616 | tf_op jit(solution)/shard_map/ppermute | solution.py:240
  20.0 17.0 %collective-permute-start.1 = (f32[272,1,128]{2,1,0:T(1,128)S(1)}, f32[272,1,128]{2,1,0:T(1,128)S(1)}, u32[]{:S(2)}, u32[]{:S(2)}) collective-permute-start(f32[272,1,128]{2,1,0:T(1,128)S(1)} %all_to_all.10.terms_ref), channel_id=1, source_target_pairs={{0,1},{1,0},{2,3},{3,2},{4,5},{5,4},{6,7},{7,6},{8,9},{9,8},{10,11... | collective-permute-start | bytes 417800 | tf_op jit(solution)/shard_map/ppermute | solution.py:254

commit v6 on v5

--- a/solution.py
+++ b/solution.py
@@ -50,6 +50,10 @@
         inside = inside + jnp.where(here, moved, 0.0)
         across = across + jnp.where(here, 0.0, moved)
     return inside + pltpu.roll(across, rows - 1, 0)
+
+
+def send_order(peers):
+    return list(range(peers))[::-1]
 
 
 def lane_lookup(row, lanes):
@@ -135,11 +139,11 @@
 
 def terms_kernel(own_ref, other_ref, offsets_ref, look_ref, turn_ref, out_ref, words_ref):
     tops = pack(own_ref[0] + other_ref[0], own_ref[1] + other_ref[1], words_ref)
-    for slab in range(offsets_ref.shape[0]):
+    for place, slab in enumerate(send_order(offsets_ref.shape[0])):
         real, imag = look_up(words_ref, tops, offsets_ref[slab])
         cosine = turn_ref[0, slab : slab + 1]
         sine = turn_ref[1, slab : slab + 1]
-        first = slab * CHUNK
+        first = place * CHUNK
         out_ref[first : first + ROWS_DEV, 0, :] = cosine * real - sine * imag
         out_ref[first + ROWS_DEV : first + 2 * ROWS_DEV, 0, :] = sine * real + cosine * imag
         out_ref[first + 2 * ROWS_DEV] = look_ref[slab : slab + 1]
@@ -147,7 +151,8 @@
 
 def chunk_parts(terms_ref, part):
     first = part * ROWS_DEV
-    starts = range(first, terms_ref.shape[0], CHUNK)
+    places = send_order(terms_ref.shape[0] // CHUNK)
+    starts = [places.index(pulse) * CHUNK + first for pulse in range(len(places))]
     return [terms_ref[start : start + ROWS_DEV, 0, :] for start in starts]
 
 
@@ -156,7 +161,8 @@
     copies = sums_ref.shape[0] // pulses
     reals = chunk_parts(terms_ref, 0)
     imags = chunk_parts(terms_ref, 1)
-    looks = [terms_ref[p * CHUNK + 2 * ROWS_DEV] for p in range(pulses)]
+    places = send_order(pulses)
+    looks = [terms_ref[places.index(p) * CHUNK + 2 * ROWS_DEV] for p in range(pulses)]
     real = sum(reals[1:], reals[0])
     imag = sum(imags[1:], imags[0])
     image_ref[0] = real
@@ -250,7 +256,9 @@
         table, other_table, own_offsets, own_look, turn,
         name="terms", scratch=[pltpu.VMEM(table_shape[1:], i32)],
     )
-    terms = lax.all_to_all(terms, "pulse", 0, 0, tiled=True)
+    terms = lax.all_to_all(
+        terms, "pulse", 0, 0, tiled=True, axis_index_groups=[send_order(pulses)]
+    )
     other_terms = lax.ppermute(terms, "band", swap)
     half, sums = on_device(
         image_kernel, [(half_shape, f32), ((pulses * tiles * bands, 1, LANES), f32)], terms, name="image_sums"

time: 38 us -> 37.1 us (0.976)
  blocking collectives: 29.2 us -> 28.7 us
    all_to_all x1, blocking collectives: 14.4 us -> 12.3 us  [local(): lax.all_to_all(terms, 'pulse', 0, 0, tiled=True, axis_index_groups=[send_...]
    all_to_all x1, blocking collectives: 14.8 us -> 16.4 us  [local(): sums = lax.all_to_all(sums, ('band', 'tile', 'pulse'), 0, 0, tiled=True)]
    ppermute x1, starting transfers between devices: 1.78 us -> 1.4 us  [local(): other_terms = lax.ppermute(terms, 'band', swap)]
where the time goes in v6:
time: 37.1 us; the launch traced here: 36.8 us
  blocking collectives  28.7 us (77%)
  Pallas kernels  3.76 us (10%)
  starting transfers between devices  2.9 us (8%)
  between operations  1.3 us (4%)
    all_to_all x1, blocking collectives, local(): sums = lax.all_to_all(sums, ('band', 'tile', 'pulse'), 0, 0, tiled=True)  16.4 us
    all_to_all x1, blocking collectives, local(): lax.all_to_all(terms, 'pulse', 0, 0, tiled=True, axis_index_groups=[send_...  12.3 us
    pallas_call x5, Pallas kernels, on_device(): pl.pallas_call(kernel, out_shape=tuple((jax.ShapeDtypeStruct(shape, dtype...  3.76 us
    ppermute x1, starting transfers between devices, local(): other_table = lax.ppermute(table, 'band', swap)  1.5 us
    ppermute x1, starting transfers between devices, local(): other_terms = lax.ppermute(terms, 'band', swap)  1.4 us
  transfers between devices with their start and end apart: 2, of which 1 were waited for; matrix products, arithmetic and copies ran while one was open for 0% of the time, Pallas kernels for 1%

profile of v6, /device:TPU:1, one launch (start us, length us, event | category | flops | bytes accessed | tf_op | source)
XLA Modules:
  0.0 36.8 jit_solution(4951245956124636357)
XLA Ops:
  0.6 1.1 %table.1 = (f32[2,64,128]{2,1,0:T(8,128)S(1)}, s32[16,8,128]{2,1,0:T(8,128)S(1)}, f32[1,4096]{1,0:T(1,128)S(1)}) custom-call(bf16[2,8192]{1,0:T(2,128)(2,1)} %bitcast.3, s32[1,8,4096]{2,1,0:T(8,128)} %offsets_hbm.1, f32[1,4096]{1,0:T(1,128)} %look_hbm.1), custom_call_target="tpu_custom_call" | custom-call | bytes 1048576 | tf_op jit(solution)/shard_map/table/pallas_call | solution.py:212
  1.8 1.5 %collective-permute-start = (f32[2,64,128]{2,1,0:T(8,128)S(1)}, f32[2,64,128]{2,1,0:T(8,128)S(1)}, u32[]{:S(2)}, u32[]{:S(2)}) collective-permute-start(f32[2,64,128]{2,1,0:T(8,128)S(1)} %get-tuple-element.11.own_ref), channel_id=1, source_target_pairs={{0,1},{1,0},{2,3},{3,2},{4,5},{5,4},{6,7},{7,6},{8,9},{9,8},{10,11... | collective-permute-start | bytes 196616 | tf_op jit(solution)/shard_map/ppermute | solution.py:246
  4.0 0.2 collective-permute-done.other_ref
  4.2 1.4 %terms.1 = f32[272,1,128]{2,1,0:T(1,128)S(1)} custom-call(f32[2,64,128]{2,1,0:T(8,128)S(1)} %get-tuple-element.11.own_ref, f32[2,64,128]{2,1,0:T(8,128)S(1)} %collective-permute-done.other_ref, s32[16,8,128]{2,1,0:T(8,128)S(1)} %get-tuple-element.12.offsets_ref, f32[16,128]{1,0:T(8,128)S(1)} %get-tuple-element.14.look_ref, ...), custom_call_target="tpu_custom_call" | custom-call | bytes 1048576 | tf_op jit(solution)/shard_map/terms/pallas_call | solution.py:212
  5.6 12.3 %all_to_all.10.terms_ref = f32[272,1,128]{2,1,0:T(1,128)S(1)} all-to-all(f32[272,1,128]{2,1,0:T(1,128)S(1)} %terms.1), channel_id=1, replica_groups={{120,112,104,96,88,80,72,64,56,48,40,32,24,16,8,0},{121,113,105,97,89,8..., dimensions={0} | all-to-all | bytes 278528 | tf_op jit(solution)/shard_map/all_to_all | solution.py:259
  17.9 1.4 %collective-permute-start.1 = (f32[272,1,128]{2,1,0:T(1,128)S(1)}, f32[272,1,128]{2,1,0:T(1,128)S(1)}, u32[]{:S(2)}, u32[]{:S(2)}) collective-permute-start(f32[272,1,128]{2,1,0:T(1,128)S(1)} %all_to_all.10.terms_ref), channel_id=1, source_target_pairs={{0,1},{1,0},{2,3},{3,2},{4,5},{5,4},{6,7},{7,6},{8,9},{9,8},{10,11... | collective-permute-start | bytes 417800 | tf_op jit(solution)/shard_map/ppermute | solution.py:262
  19.3 0.3 image_sums.1
  19.6 16.4 %all_to_all.11.refs_2_ = f32[128,1,128]{2,1,0:T(1,128)S(1)} all-to-all(f32[128,1,128]{2,1,0:T(1,128)S(1)} %get-tuple-element.17), channel_id=1, replica_groups=mesh['pulse'=16,'tile'=4,'band'=2] {'band','tile','pulse'}, dimensions={0} | all-to-all | bytes 131072 | tf_op jit(solution)/shard_map/all_to_all | solution.py:266
  36.0 0.0 collective-permute-done.1.refs_1_
  36.0 0.8 %gradient.1 = (f32[1,128]{1,0:T(1,128)}, f32[2,8,256]{2,1,0:T(8,128)}) custom-call(f32[2,8,128]{2,1,0:T(8,128)S(1)} %get-tuple-element.16.refs_0_, f32[272,1,128]{2,1,0:T(1,128)S(1)} %collective-permute-done.1.refs_1_, f32[128,1,128]{2,1,0:T(1,128)S(1)} %all_to_all.11.refs_2_), custom_call_target="tpu_custom_call" | custom-call | bytes 1048576 | tf_op jit(solution)/shard_map/gradient/pallas_call | solution.py:212
  (1 shorter events, 0.0 us)
Async XLA Ops:
  1.8 2.4 %collective-permute-start = (f32[2,64,128]{2,1,0:T(8,128)S(1)}, f32[2,64,128]{2,1,0:T(8,128)S(1)}, u32[]{:S(2)}, u32[]{:S(2)}) collective-permute-start(f32[2,64,128]{2,1,0:T(8,128)S(1)} %get-tuple-element.11.own_ref), channel_id=1, source_target_pairs={{0,1},{1,0},{2,3},{3,2},{4,5},{5,4},{6,7},{7,6},{8,9},{9,8},{10,11... | collective-permute-start | bytes 196616 | tf_op jit(solution)/shard_map/ppermute | solution.py:246
  17.9 18.2 %collective-permute-start.1 = (f32[272,1,128]{2,1,0:T(1,128)S(1)}, f32[272,1,128]{2,1,0:T(1,128)S(1)}, u32[]{:S(2)}, u32[]{:S(2)}) collective-permute-start(f32[272,1,128]{2,1,0:T(1,128)S(1)} %all_to_all.10.terms_ref), channel_id=1, source_target_pairs={{0,1},{1,0},{2,3},{3,2},{4,5},{5,4},{6,7},{7,6},{8,9},{9,8},{10,11... | collective-permute-start | bytes 417800 | tf_op jit(solution)/shard_map/ppermute | solution.py:262

commit v7 on v6

--- a/solution.py
+++ b/solution.py
@@ -66,11 +66,7 @@
         pltpu.make_async_copy(echo_hbm, echo_ref, arrived.at[0]),
         pltpu.make_async_copy(look_hbm, look_ref, arrived.at[1]),
     ]
-    for slab in range(offsets_ref.shape[0]):
-        block = pl.ds(pl.multiple_of((2 * slab + band) * LANES, LANES), LANES)
-        copies.append(
-            pltpu.make_async_copy(offsets_hbm.at[0, :, block], offsets_ref.at[slab], arrived.at[2 + slab])
-        )
+    copies.append(pltpu.make_async_copy(offsets_hbm, offsets_ref, arrived.at[2]))
     for copy in copies:
         copy.start()
     lane = lax.broadcasted_iota(jnp.int32, (1, LANES), 1)
@@ -98,29 +94,20 @@
 
 
 def pack(real, imag, words_ref):
-    rows = real.shape[0]
-    size = jnp.maximum(jnp.abs(real), jnp.abs(imag))
-    lane = lax.broadcasted_iota(jnp.int32, size.shape, 1)
-    row = lax.broadcasted_iota(jnp.int32, size.shape, 0)
-    first_half = lane < LANES // 2
-    tops = []
-    for half in range(2):
-        inside = first_half if half == 0 else jnp.logical_not(first_half)
-        top = jnp.max(jnp.where(inside, size, 0.0), axis=1, keepdims=True)
-        tops.append(jnp.where(top > 0.0, top, 1.0))
-    shrink = jnp.where(first_half, 1.0 / tops[0], 1.0 / tops[1])
+    top = jnp.max(jnp.maximum(jnp.abs(real), jnp.abs(imag)), axis=0, keepdims=True)
+    top = jnp.where(top > 0.0, top, 1.0)
+    shrink = 1.0 / top
     real = jnp.floor(real * shrink * MOST + 0.5).astype(jnp.int32)
     imag = jnp.floor(imag * shrink * MOST + 0.5).astype(jnp.int32)
     words_ref[...] = (real << 16) | (imag & 0xFFFF)
-    spread = jnp.where(lane == row, tops[0], 0.0) + jnp.where(lane == row + rows, tops[1], 0.0)
-    return jnp.sum(spread, axis=0, keepdims=True)
+    return top
 
 
 def look_up(words_ref, tops, offsets):
     rows = words_ref.shape[0]
     lanes = offsets & (LANES - 1)
     high = offsets >> 7
-    top = lane_lookup(jnp.broadcast_to(tops, offsets.shape), high + ((offsets & 64) * (rows // 64)))
+    top = lane_lookup(jnp.broadcast_to(tops, offsets.shape), lanes)
     low = high & (CHAIN - 1)
     chains = [None] * (rows // CHAIN)
     for step in range(CHAIN):
@@ -139,8 +126,10 @@
 
 def terms_kernel(own_ref, other_ref, offsets_ref, look_ref, turn_ref, out_ref, words_ref):
     tops = pack(own_ref[0] + other_ref[0], own_ref[1] + other_ref[1], words_ref)
-    for place, slab in enumerate(send_order(offsets_ref.shape[0])):
-        real, imag = look_up(words_ref, tops, offsets_ref[slab])
+    band = lax.axis_index("band")
+    for place, slab in enumerate(send_order(look_ref.shape[0])):
+        block = pl.ds(pl.multiple_of((2 * slab + band) * LANES, LANES), LANES)
+        real, imag = look_up(words_ref, tops, offsets_ref[0, :, block])
         cosine = turn_ref[0, slab : slab + 1]
         sine = turn_ref[1, slab : slab + 1]
         first = place * CHUNK
@@ -181,7 +170,7 @@
     sums = jnp.where(lane == 0, power_cross_sums, 0.0) + jnp.where(lane == 1, cross_sums, 0.0)
     sums = sums + jnp.where(lane == 2, power_sum, 0.0) + jnp.where(lane == 3, quart_sum, 0.0)
     for copy in range(copies):
-        sums_ref[copy * pulses : (copy + 1) * pulses, 0, :] = sums
+        sums_ref[copy * pulses : (copy + 1) * pulses] = sums
 
 
 def join(own_ref, other_terms_ref, image_ref):
@@ -196,7 +185,7 @@
 
 def gradient_kernel(own_ref, other_ref, sums_ref, gradient_ref, image_ref, *, pulses, npix):
     join(own_ref, other_ref, image_ref)
-    totals = jnp.sum(sums_ref[:, 0, :], axis=0, keepdims=True)
+    totals = jnp.sum(sums_ref[...], axis=0, keepdims=True)
     mean_power = totals[:, 2:3] / npix + power_floor
     quart = totals[:, 3:4] / npix
     gradient = 2.0 * totals[:, 0:1] / (mean_power * mean_power) - 2.0 * quart * totals[:, 1:2] / (
@@ -238,10 +227,10 @@
     inputs = (echo.reshape(2, bins), offsets, look)
     table, own_offsets, look = on_device(
         table_kernel,
-        [(table_shape, f32), ((slabs, rows_dev, LANES), i32), ((1, columns), f32)],
+        [(table_shape, f32), ((1, rows_dev, columns), i32), ((1, columns), f32)],
         *(pltpu.with_memory_space_constraint(array, pltpu.HBM) for array in inputs),
         name="table", spaces=[HBM] * 3,
-        scratch=[pltpu.VMEM((2, bins), echo.dtype), pltpu.SemaphoreType.DMA((2 + slabs,))],
+        scratch=[pltpu.VMEM((2, bins), echo.dtype), pltpu.SemaphoreType.DMA((3,))],
     )
     other_table = lax.ppermute(table, "band", swap)
     own_look, turn = on_device(
@@ -261,7 +250,7 @@
     )
     other_terms = lax.ppermute(terms, "band", swap)
     half, sums = on_device(
-        image_kernel, [(half_shape, f32), ((pulses * tiles * bands, 1, LANES), f32)], terms, name="image_sums"
+        image_kernel, [(half_shape, f32), ((pulses * tiles * bands, LANES), f32)], terms, name="image_sums"
     )
     sums = lax.all_to_all(sums, ("band", "tile", "pulse"), 0, 0, tiled=True)
     gradient, image = on_device(

time: 37.1 us -> 36.7 us (0.989)
  no operation moved by 1% of the time
where the time goes in v7:
time: 36.7 us; the launch traced here: 36.5 us
  blocking collectives  28.7 us (78%)
  Pallas kernels  3.41 us (9%)
  starting transfers between devices  2.9 us (8%)
  between operations  1.3 us (4%)
    all_to_all x1, blocking collectives, local(): sums = lax.all_to_all(sums, ('band', 'tile', 'pulse'), 0, 0, tiled=True)  16.4 us
    all_to_all x1, blocking collectives, local(): lax.all_to_all(terms, 'pulse', 0, 0, tiled=True, axis_index_groups=[send_...  12.3 us
    pallas_call x5, Pallas kernels, on_device(): pl.pallas_call(kernel, out_shape=tuple((jax.ShapeDtypeStruct(shape, dtype...  3.41 us
    ppermute x1, starting transfers between devices, local(): other_table = lax.ppermute(table, 'band', swap)  1.5 us
    ppermute x1, starting transfers between devices, local(): other_terms = lax.ppermute(terms, 'band', swap)  1.4 us
  transfers between devices with their start and end apart: 2, of which 1 were waited for; matrix products, arithmetic and copies ran while one was open for 0% of the time, Pallas kernels for 1%

profile of v7, /device:TPU:1, one launch (start us, length us, event | category | flops | bytes accessed | tf_op | source)
XLA Modules:
  0.0 36.5 jit_solution(13920462470727812063)
XLA Ops:
  0.6 1.0 %table.1 = (f32[2,64,128]{2,1,0:T(8,128)S(1)}, s32[1,8,4096]{2,1,0:T(8,128)S(1)}, f32[1,4096]{1,0:T(1,128)S(1)}) custom-call(bf16[2,8192]{1,0:T(2,128)(2,1)} %bitcast.9, s32[1,8,4096]{2,1,0:T(8,128)} %offsets_hbm.1, f32[1,4096]{1,0:T(1,128)} %look_hbm.1), custom_call_target="tpu_custom_call" | custom-call | bytes 1048576 | tf_op jit(solution)/shard_map/table/pallas_call | solution.py:201
  1.6 1.5 %collective-permute-start = (f32[2,64,128]{2,1,0:T(8,128)S(1)}, f32[2,64,128]{2,1,0:T(8,128)S(1)}, u32[]{:S(2)}, u32[]{:S(2)}) collective-permute-start(f32[2,64,128]{2,1,0:T(8,128)S(1)} %get-tuple-element.11.own_ref), channel_id=1, source_target_pairs={{0,1},{1,0},{2,3},{3,2},{4,5},{5,4},{6,7},{7,6},{8,9},{9,8},{10,11... | collective-permute-start | bytes 196616 | tf_op jit(solution)/shard_map/ppermute | solution.py:235
  3.8 0.2 collective-permute-done.other_ref
  4.0 1.3 %terms.1 = f32[272,1,128]{2,1,0:T(1,128)S(1)} custom-call(f32[2,64,128]{2,1,0:T(8,128)S(1)} %get-tuple-element.11.own_ref, f32[2,64,128]{2,1,0:T(8,128)S(1)} %collective-permute-done.other_ref, s32[1,8,4096]{2,1,0:T(8,128)S(1)} %get-tuple-element.12.offsets_ref, f32[16,128]{1,0:T(8,128)S(1)} %get-tuple-element.14.look_ref, ...), custom_call_target="tpu_custom_call" | custom-call | bytes 1048576 | tf_op jit(solution)/shard_map/terms/pallas_call | solution.py:201
  5.3 12.3 %all_to_all.16.terms_ref = f32[272,1,128]{2,1,0:T(1,128)S(1)} all-to-all(f32[272,1,128]{2,1,0:T(1,128)S(1)} %terms.1), channel_id=1, replica_groups={{120,112,104,96,88,80,72,64,56,48,40,32,24,16,8,0},{121,113,105,97,89,8..., dimensions={0} | all-to-all | bytes 278528 | tf_op jit(solution)/shard_map/all_to_all | solution.py:248
  17.6 1.4 %collective-permute-start.1 = (f32[272,1,128]{2,1,0:T(1,128)S(1)}, f32[272,1,128]{2,1,0:T(1,128)S(1)}, u32[]{:S(2)}, u32[]{:S(2)}) collective-permute-start(f32[272,1,128]{2,1,0:T(1,128)S(1)} %all_to_all.16.terms_ref), channel_id=1, source_target_pairs={{0,1},{1,0},{2,3},{3,2},{4,5},{5,4},{6,7},{7,6},{8,9},{9,8},{10,11... | collective-permute-start | bytes 417800 | tf_op jit(solution)/shard_map/ppermute | solution.py:251
  19.0 0.3 image_sums.1
  19.3 16.4 %all_to_all.17 = f32[128,1,128]{2,1,0:T(1,128)S(1)} all-to-all(f32[128,1,128]{2,1,0:T(1,128)S(1)} %bitcast.8), channel_id=1, replica_groups=mesh['pulse'=16,'tile'=4,'band'=2] {'band','tile','pulse'}, dimensions={0} | all-to-all | bytes 131072 | tf_op jit(solution)/shard_map/all_to_all | solution.py:255
  35.7 0.0 collective-permute-done.1.refs_1_
  35.7 0.8 %gradient.1 = (f32[1,128]{1,0:T(1,128)}, f32[2,8,256]{2,1,0:T(8,128)}) custom-call(f32[2,8,128]{2,1,0:T(8,128)S(1)} %get-tuple-element.16.refs_0_, f32[272,1,128]{2,1,0:T(1,128)S(1)} %collective-permute-done.1.refs_1_, f32[128,128]{1,0:T(8,128)S(1)} %bitcast.7), custom_call_target="tpu_custom_call" | custom-call | bytes 1048576 | tf_op jit(solution)/shard_map/gradient/pallas_call | solution.py:201
  (1 shorter events, 0.0 us)
Async XLA Ops:
  1.6 2.4 %collective-permute-start = (f32[2,64,128]{2,1,0:T(8,128)S(1)}, f32[2,64,128]{2,1,0:T(8,128)S(1)}, u32[]{:S(2)}, u32[]{:S(2)}) collective-permute-start(f32[2,64,128]{2,1,0:T(8,128)S(1)} %get-tuple-element.11.own_ref), channel_id=1, source_target_pairs={{0,1},{1,0},{2,3},{3,2},{4,5},{5,4},{6,7},{7,6},{8,9},{9,8},{10,11... | collective-permute-start | bytes 196616 | tf_op jit(solution)/shard_map/ppermute | solution.py:235
  17.6 18.1 %collective-permute-start.1 = (f32[272,1,128]{2,1,0:T(1,128)S(1)}, f32[272,1,128]{2,1,0:T(1,128)S(1)}, u32[]{:S(2)}, u32[]{:S(2)}) collective-permute-start(f32[272,1,128]{2,1,0:T(1,128)S(1)} %all_to_all.16.terms_ref), channel_id=1, source_target_pairs={{0,1},{1,0},{2,3},{3,2},{4,5},{5,4},{6,7},{7,6},{8,9},{9,8},{10,11... | collective-permute-start | bytes 417800 | tf_op jit(solution)/shard_map/ppermute | solution.py:251

commit v8 on v7

--- a/solution.py
+++ b/solution.py
@@ -133,16 +133,16 @@
         cosine = turn_ref[0, slab : slab + 1]
         sine = turn_ref[1, slab : slab + 1]
         first = place * CHUNK
-        out_ref[first : first + ROWS_DEV, 0, :] = cosine * real - sine * imag
-        out_ref[first + ROWS_DEV : first + 2 * ROWS_DEV, 0, :] = sine * real + cosine * imag
-        out_ref[first + 2 * ROWS_DEV] = look_ref[slab : slab + 1]
+        out_ref[first : first + ROWS_DEV] = cosine * real - sine * imag
+        out_ref[first + ROWS_DEV : first + 2 * ROWS_DEV] = sine * real + cosine * imag
+        out_ref[first + 2 * ROWS_DEV : first + CHUNK] = look_ref[slab : slab + 1]
 
 
 def chunk_parts(terms_ref, part):
     first = part * ROWS_DEV
     places = send_order(terms_ref.shape[0] // CHUNK)
     starts = [places.index(pulse) * CHUNK + first for pulse in range(len(places))]
-    return [terms_ref[start : start + ROWS_DEV, 0, :] for start in starts]
+    return [terms_ref[start : start + ROWS_DEV] for start in starts]
 
 
 def image_kernel(terms_ref, image_ref, sums_ref):
@@ -151,7 +151,8 @@
     reals = chunk_parts(terms_ref, 0)
     imags = chunk_parts(terms_ref, 1)
     places = send_order(pulses)
-    looks = [terms_ref[places.index(p) * CHUNK + 2 * ROWS_DEV] for p in range(pulses)]
+    firsts = [places.index(p) * CHUNK + 2 * ROWS_DEV for p in range(pulses)]
+    looks = [terms_ref[first : first + 1] for first in firsts]
     real = sum(reals[1:], reals[0])
     imag = sum(imags[1:], imags[0])
     image_ref[0] = real
@@ -241,13 +242,13 @@
     )
     (terms,) = on_device(
         terms_kernel,
-        [((slabs * CHUNK, 1, LANES), f32)],
+        [((slabs * CHUNK, LANES), f32)],
         table, other_table, own_offsets, own_look, turn,
         name="terms", scratch=[pltpu.VMEM(table_shape[1:], i32)],
     )
     terms = lax.all_to_all(
-        terms, "pulse", 0, 0, tiled=True, axis_index_groups=[send_order(pulses)]
-    )
+        terms.reshape(-1, 1, LANES), "pulse", 0, 0, tiled=True, axis_index_groups=[send_order(pulses)]
+    ).reshape(-1, LANES)
     other_terms = lax.ppermute(terms, "band", swap)
     half, sums = on_device(
         image_kernel, [(half_shape, f32), ((pulses * tiles * bands, LANES), f32)], terms, name="image_sums"

time: 36.7 us -> 36.4 us (level)
  no operation moved by 1% of the time
where the time goes in v8:
time: 36.4 us; the launch traced here: 36.3 us
  blocking collectives  28.7 us (79%)
  Pallas kernels  3.2 us (9%)
  starting transfers between devices  2.9 us (8%)
  between operations  1.3 us (4%)
    all_to_all x1, blocking collectives, local(): sums = lax.all_to_all(sums, ('band', 'tile', 'pulse'), 0, 0, tiled=True)  16.4 us
    all_to_all x1, blocking collectives, local(): lax.all_to_all(terms.reshape(-1, 1, LANES), 'pulse', 0, 0, tiled=True, ax...  12.3 us
    pallas_call x5, Pallas kernels, on_device(): pl.pallas_call(kernel, out_shape=tuple((jax.ShapeDtypeStruct(shape, dtype...  3.2 us
    ppermute x1, starting transfers between devices, local(): other_table = lax.ppermute(table, 'band', swap)  1.5 us
    ppermute x1, starting transfers between devices, local(): other_terms = lax.ppermute(terms, 'band', swap)  1.4 us
  transfers between devices with their start and end apart: 2, of which 1 were waited for; matrix products, arithmetic and copies ran while one was open for 0% of the time, Pallas kernels for 1%

profile of v8, /device:TPU:1, one launch (start us, length us, event | category | flops | bytes accessed | tf_op | source)
XLA Modules:
  0.0 36.3 jit_solution(6537867642387278971)
XLA Ops:
  0.6 1.0 %table.1 = (f32[2,64,128]{2,1,0:T(8,128)S(1)}, s32[1,8,4096]{2,1,0:T(8,128)S(1)}, f32[1,4096]{1,0:T(1,128)S(1)}) custom-call(bf16[2,8192]{1,0:T(2,128)(2,1)} %bitcast.16, s32[1,8,4096]{2,1,0:T(8,128)} %offsets_hbm.1, f32[1,4096]{1,0:T(1,128)} %look_hbm.1), custom_call_target="tpu_custom_call" | custom-call | bytes 1048576 | tf_op jit(solution)/shard_map/table/pallas_call | solution.py:202
  1.6 1.5 %collective-permute-start = (f32[2,64,128]{2,1,0:T(8,128)S(1)}, f32[2,64,128]{2,1,0:T(8,128)S(1)}, u32[]{:S(2)}, u32[]{:S(2)}) collective-permute-start(f32[2,64,128]{2,1,0:T(8,128)S(1)} %get-tuple-element.11.own_ref), channel_id=1, source_target_pairs={{0,1},{1,0},{2,3},{3,2},{4,5},{5,4},{6,7},{7,6},{8,9},{9,8},{10,11... | collective-permute-start | bytes 196616 | tf_op jit(solution)/shard_map/ppermute | solution.py:236
  3.8 0.2 collective-permute-done.other_ref
  4.0 1.3 %terms.1 = f32[272,128]{1,0:T(8,128)S(1)} custom-call(f32[2,64,128]{2,1,0:T(8,128)S(1)} %get-tuple-element.11.own_ref, f32[2,64,128]{2,1,0:T(8,128)S(1)} %collective-permute-done.other_ref, s32[1,8,4096]{2,1,0:T(8,128)S(1)} %get-tuple-element.12.offsets_ref, f32[16,128]{1,0:T(8,128)S(1)} %get-tuple-element.14.look_ref, ...), custom_call_target="tpu_custom_call" | custom-call | bytes 1048576 | tf_op jit(solution)/shard_map/terms/pallas_call | solution.py:202
  5.3 12.3 %all_to_all.16 = f32[272,1,128]{2,1,0:T(1,128)S(1)} all-to-all(f32[272,1,128]{2,1,0:T(1,128)S(1)} %bitcast.13), channel_id=1, replica_groups={{120,112,104,96,88,80,72,64,56,48,40,32,24,16,8,0},{121,113,105,97,89,8..., dimensions={0} | all-to-all | bytes 278528 | tf_op jit(solution)/shard_map/all_to_all | solution.py:249
  17.5 1.4 %collective-permute-start.1 = (f32[272,128]{1,0:T(8,128)S(1)}, f32[272,128]{1,0:T(8,128)S(1)}, u32[]{:S(2)}, u32[]{:S(2)}) collective-permute-start(f32[272,128]{1,0:T(8,128)S(1)} %bitcast.11), channel_id=1, source_target_pairs={{0,1},{1,0},{2,3},{3,2},{4,5},{5,4},{6,7},{7,6},{8,9},{9,8},{10,11... | collective-permute-start | bytes 417800 | tf_op jit(solution)/shard_map/ppermute | solution.py:252
  18.9 0.1 image_sums.1
  19.1 16.4 %all_to_all.17 = f32[128,1,128]{2,1,0:T(1,128)S(1)} all-to-all(f32[128,1,128]{2,1,0:T(1,128)S(1)} %bitcast.15), channel_id=1, replica_groups=mesh['pulse'=16,'tile'=4,'band'=2] {'band','tile','pulse'}, dimensions={0} | all-to-all | bytes 131072 | tf_op jit(solution)/shard_map/all_to_all | solution.py:256
  35.5 0.0 collective-permute-done.1.refs_1_
  35.5 0.8 %gradient.1 = (f32[1,128]{1,0:T(1,128)}, f32[2,8,256]{2,1,0:T(8,128)}) custom-call(f32[2,8,128]{2,1,0:T(8,128)S(1)} %get-tuple-element.16.refs_0_, f32[272,128]{1,0:T(8,128)S(1)} %collective-permute-done.1.refs_1_, f32[128,128]{1,0:T(8,128)S(1)} %bitcast.14), custom_call_target="tpu_custom_call" | custom-call | bytes 1048576 | tf_op jit(solution)/shard_map/gradient/pallas_call | solution.py:202
  (1 shorter events, 0.0 us)
Async XLA Ops:
  1.6 2.4 %collective-permute-start = (f32[2,64,128]{2,1,0:T(8,128)S(1)}, f32[2,64,128]{2,1,0:T(8,128)S(1)}, u32[]{:S(2)}, u32[]{:S(2)}) collective-permute-start(f32[2,64,128]{2,1,0:T(8,128)S(1)} %get-tuple-element.11.own_ref), channel_id=1, source_target_pairs={{0,1},{1,0},{2,3},{3,2},{4,5},{5,4},{6,7},{7,6},{8,9},{9,8},{10,11... | collective-permute-start | bytes 196616 | tf_op jit(solution)/shard_map/ppermute | solution.py:236
  17.5 18.0 %collective-permute-start.1 = (f32[272,128]{1,0:T(8,128)S(1)}, f32[272,128]{1,0:T(8,128)S(1)}, u32[]{:S(2)}, u32[]{:S(2)}) collective-permute-start(f32[272,128]{1,0:T(8,128)S(1)} %bitcast.11), channel_id=1, source_target_pairs={{0,1},{1,0},{2,3},{3,2},{4,5},{5,4},{6,7},{7,6},{8,9},{9,8},{10,11... | collective-permute-start | bytes 417800 | tf_op jit(solution)/shard_map/ppermute | solution.py:252

commit v9 on v8

--- a/solution.py
+++ b/solution.py
@@ -73,10 +73,9 @@
     phase_index = (lane * (5 + 2 * band)) & 63
     sine, cosine = sine_cosine(phase_index.astype(jnp.float32) * (math.pi / 32.0))
     copies[0].wait()
-    filt = []
-    for part in range(2):
-        rows = echo_ref[part : part + 1].astype(jnp.float32).reshape(table_ref.shape[1], LANES)
-        filt.append(filtered_rows(rows))
+    rows = table_ref.shape[1]
+    both = filtered_rows(echo_ref[...].astype(jnp.float32).reshape(2 * rows, LANES))
+    filt = both[:rows], both[rows:]
     table_ref[0] = cosine * filt[0] - sine * filt[1]
     table_ref[1] = sine * filt[0] + cosine * filt[1]
     for copy in copies[1:]:

time: 36.4 us -> 36.4 us (level)
  no operation moved by 1% of the time
where the time goes in v9:
time: 36.4 us; the launch traced here: 36.3 us
  blocking collectives  28.7 us (79%)
  Pallas kernels  3.2 us (9%)
  starting transfers between devices  2.9 us (8%)
  between operations  1.3 us (4%)
    all_to_all x1, blocking collectives, local(): sums = lax.all_to_all(sums, ('band', 'tile', 'pulse'), 0, 0, tiled=True)  16.4 us
    all_to_all x1, blocking collectives, local(): lax.all_to_all(terms.reshape(-1, 1, LANES), 'pulse', 0, 0, tiled=True, ax...  12.3 us
    pallas_call x5, Pallas kernels, on_device(): pl.pallas_call(kernel, out_shape=tuple((jax.ShapeDtypeStruct(shape, dtype...  3.2 us
    ppermute x1, starting transfers between devices, local(): other_table = lax.ppermute(table, 'band', swap)  1.5 us
    ppermute x1, starting transfers between devices, local(): other_terms = lax.ppermute(terms, 'band', swap)  1.4 us
  transfers between devices with their start and end apart: 2, of which 1 were waited for; matrix products, arithmetic and copies ran while one was open for 0% of the time, Pallas kernels for 1%

profile of v9, /device:TPU:1, one launch (start us, length us, event | category | flops | bytes accessed | tf_op | source)
XLA Modules:
  0.0 36.3 jit_solution(14488095596787913051)
XLA Ops:
  0.6 1.0 %table.1 = (f32[2,64,128]{2,1,0:T(8,128)S(1)}, s32[1,8,4096]{2,1,0:T(8,128)S(1)}, f32[1,4096]{1,0:T(1,128)S(1)}) custom-call(bf16[2,8192]{1,0:T(2,128)(2,1)} %bitcast.16, s32[1,8,4096]{2,1,0:T(8,128)} %offsets_hbm.1, f32[1,4096]{1,0:T(1,128)} %look_hbm.1), custom_call_target="tpu_custom_call" | custom-call | bytes 1048576 | tf_op jit(solution)/shard_map/table/pallas_call | solution.py:201
  1.6 1.5 %collective-permute-start = (f32[2,64,128]{2,1,0:T(8,128)S(1)}, f32[2,64,128]{2,1,0:T(8,128)S(1)}, u32[]{:S(2)}, u32[]{:S(2)}) collective-permute-start(f32[2,64,128]{2,1,0:T(8,128)S(1)} %get-tuple-element.11.own_ref), channel_id=1, source_target_pairs={{0,1},{1,0},{2,3},{3,2},{4,5},{5,4},{6,7},{7,6},{8,9},{9,8},{10,11... | collective-permute-start | bytes 196616 | tf_op jit(solution)/shard_map/ppermute | solution.py:235
  3.8 0.2 collective-permute-done.other_ref
  4.0 1.3 %terms.1 = f32[272,128]{1,0:T(8,128)S(1)} custom-call(f32[2,64,128]{2,1,0:T(8,128)S(1)} %get-tuple-element.11.own_ref, f32[2,64,128]{2,1,0:T(8,128)S(1)} %collective-permute-done.other_ref, s32[1,8,4096]{2,1,0:T(8,128)S(1)} %get-tuple-element.12.offsets_ref, f32[16,128]{1,0:T(8,128)S(1)} %get-tuple-element.14.look_ref, ...), custom_call_target="tpu_custom_call" | custom-call | bytes 1048576 | tf_op jit(solution)/shard_map/terms/pallas_call | solution.py:201
  5.3 12.3 %all_to_all.16 = f32[272,1,128]{2,1,0:T(1,128)S(1)} all-to-all(f32[272,1,128]{2,1,0:T(1,128)S(1)} %bitcast.13), channel_id=1, replica_groups={{120,112,104,96,88,80,72,64,56,48,40,32,24,16,8,0},{121,113,105,97,89,8..., dimensions={0} | all-to-all | bytes 278528 | tf_op jit(solution)/shard_map/all_to_all | solution.py:248
  17.6 1.4 %collective-permute-start.1 = (f32[272,128]{1,0:T(8,128)S(1)}, f32[272,128]{1,0:T(8,128)S(1)}, u32[]{:S(2)}, u32[]{:S(2)}) collective-permute-start(f32[272,128]{1,0:T(8,128)S(1)} %bitcast.11), channel_id=1, source_target_pairs={{0,1},{1,0},{2,3},{3,2},{4,5},{5,4},{6,7},{7,6},{8,9},{9,8},{10,11... | collective-permute-start | bytes 417800 | tf_op jit(solution)/shard_map/ppermute | solution.py:251
  18.9 0.1 image_sums.1
  19.1 16.4 %all_to_all.17 = f32[128,1,128]{2,1,0:T(1,128)S(1)} all-to-all(f32[128,1,128]{2,1,0:T(1,128)S(1)} %bitcast.15), channel_id=1, replica_groups=mesh['pulse'=16,'tile'=4,'band'=2] {'band','tile','pulse'}, dimensions={0} | all-to-all | bytes 131072 | tf_op jit(solution)/shard_map/all_to_all | solution.py:255
  35.5 0.0 collective-permute-done.1.refs_1_
  35.5 0.8 %gradient.1 = (f32[1,128]{1,0:T(1,128)}, f32[2,8,256]{2,1,0:T(8,128)}) custom-call(f32[2,8,128]{2,1,0:T(8,128)S(1)} %get-tuple-element.16.refs_0_, f32[272,128]{1,0:T(8,128)S(1)} %collective-permute-done.1.refs_1_, f32[128,128]{1,0:T(8,128)S(1)} %bitcast.14), custom_call_target="tpu_custom_call" | custom-call | bytes 1048576 | tf_op jit(solution)/shard_map/gradient/pallas_call | solution.py:201
  (1 shorter events, 0.0 us)
Async XLA Ops:
  1.6 2.4 %collective-permute-start = (f32[2,64,128]{2,1,0:T(8,128)S(1)}, f32[2,64,128]{2,1,0:T(8,128)S(1)}, u32[]{:S(2)}, u32[]{:S(2)}) collective-permute-start(f32[2,64,128]{2,1,0:T(8,128)S(1)} %get-tuple-element.11.own_ref), channel_id=1, source_target_pairs={{0,1},{1,0},{2,3},{3,2},{4,5},{5,4},{6,7},{7,6},{8,9},{9,8},{10,11... | collective-permute-start | bytes 196616 | tf_op jit(solution)/shard_map/ppermute | solution.py:235
  17.6 18.0 %collective-permute-start.1 = (f32[272,128]{1,0:T(8,128)S(1)}, f32[272,128]{1,0:T(8,128)S(1)}, u32[]{:S(2)}, u32[]{:S(2)}) collective-permute-start(f32[272,128]{1,0:T(8,128)S(1)} %bitcast.11), channel_id=1, source_target_pairs={{0,1},{1,0},{2,3},{3,2},{4,5},{5,4},{6,7},{7,6},{8,9},{9,8},{10,11... | collective-permute-start | bytes 417800 | tf_op jit(solution)/shard_map/ppermute | solution.py:251
